TPU v7x, 512 devices: a whole 4x4x16 slice. The times are simulated.
512 devices in a mesh: tm: 16 (over y, z_hi), space: 32 (over z_lo, x, core).
Axes of the slice: x: 4, y: 4, z: 16 (z_hi: 4, z_lo: 4; z = z_hi * 4 + z_lo), core: 2. Of those that a mesh axis runs over, the one named last changes fastest.
Arguments:
- node_states: float32 [16, 3, 64, 128, 128], P('tm', None, None, 'space'), may hold values from -6 to 6
- initial_state: float32 [64, 128, 128], P(None, 'space'), may hold values from -6 to 6
- velocity: bfloat16 [3, 64, 128, 128], P(None, None, 'space'), may hold values from -1 to 1
Outputs:
- new_states: float32 [16, 3, 64, 128, 128], P('tm', None, None, 'space')
All inputs are finite; a program needn't handle non-finite values.
Results may differ from a plain program's by a relative error of at most 0.0003.
Values sent between devices are 32-bit elements; how exact they have to be, the bound alone decides.
A program may use at most 64 MiB of HBM per device.

v0:
```python
import jax
import jax.numpy as jnp
import numpy as np
from jax import lax
from jax.sharding import PartitionSpec as P

CZ = 16
SWEEPS = 3


slice_step = 0.08
fine_lift = 6.0
coarse_lift = 1.0
highest = lax.Precision.HIGHEST


def extended(value, sides, width):
    for axis, dim in sides:
        devices, length = (lax.axis_size(axis), value.shape[dim])
        up = [(i, (i + 1) % devices) for i in range(devices - 1)]
        down = [(j, i) for i, j in up]
        last = lax.slice_in_dim(value, length - width, length, axis=dim)
        initial = lax.slice_in_dim(value, 0, width, axis=dim)
        before = lax.ppermute(last, axis, up)
        after = lax.ppermute(initial, axis, down)
        value = jnp.concatenate([before, value, after], axis=dim)
    return value


def passed_along(block, axis, distance):
    devices = range(lax.axis_size(axis))
    route = [(i - distance, i) for i in devices if i - distance in devices]
    return lax.ppermute(block, axis, route)


def lagrange_derivative(points):
    number = len(points)
    bary_weights = np.array(
        [
            1.0
            / np.prod(
                [points[col_index] - points[other] for other in range(number) if other != col_index]
            )
            for col_index in range(number)
        ]
    )
    derivative = np.zeros((number, number))
    for row_index in range(number):
        for col_index in range(number):
            if row_index != col_index:
                derivative[row_index, col_index] = (
                    bary_weights[col_index]
                    / bary_weights[row_index]
                    / (points[row_index] - points[col_index])
                )
        derivative[row_index, row_index] = -np.sum(derivative[row_index])
    return derivative


def gradient_table(points):
    derivative = lagrange_derivative(points)
    identity = np.eye(len(points))
    stacked = np.concatenate(
        [
            np.kron(np.kron(derivative, identity), identity),
            np.kron(np.kron(identity, derivative), identity),
            np.kron(np.kron(identity, identity), derivative),
        ],
        axis=0,
    )
    return jnp.asarray(stacked, dtype=jnp.float32)


def level_tables():
    points = np.array([-1.0, -1.0 / np.sqrt(5.0), 1.0 / np.sqrt(5.0), 1.0])
    weights = np.array([1.0, 5.0, 5.0, 1.0]) / 6.0
    prolong = np.stack([(1.0 - points) / 2.0, (1.0 + points) / 2.0], axis=1)
    restrict_line = prolong.T * weights[None, :]
    restrict_cube = np.kron(np.kron(restrict_line, restrict_line), restrict_line)
    prolong_cube = np.kron(np.kron(prolong, prolong), prolong)
    return (
        gradient_table(points),
        gradient_table(np.array([-1.0, 1.0])),
        jnp.asarray(restrict_cube, dtype=jnp.float32),
        jnp.asarray(prolong_cube, dtype=jnp.float32),
    )


def corner_values(flow):
    row_count = flow.shape[2]
    columns = flow.shape[3]
    return flow.reshape(3, 4, 4, 4, row_count, columns)[:, ::3, ::3, ::3].reshape(
        3, 8, row_count, columns
    )


def shift_columns(values, offset):
    zeros_pad = jnp.zeros(values.shape[:-1] + (abs(offset),), values.dtype)
    if offset > 0:
        return jnp.concatenate([zeros_pad, values[..., :-offset]], axis=-1)
    return jnp.concatenate([values[..., -offset:], zeros_pad], axis=-1)


def upwind(inside, outside, normal, lift):
    return lift * jnp.minimum(normal, 0.0) * (inside - outside)


def apply_operator(fields, flow, gradient, order, lift, lower, upper):
    number = fields.shape[0]
    row_count = fields.shape[2]
    columns = fields.shape[3]
    nodes = order**3
    far_node = order - 1
    gradients = jnp.einsum("kn,fnxe->fkxe", gradient, fields, precision=highest).reshape(
        number, 3, nodes, row_count, columns
    )
    result = -(flow[0] * gradients[:, 0] + flow[1] * gradients[:, 1] + flow[2] * gradients[:, 2])
    nodal_cube = fields.reshape(number, order, order, order, row_count, columns)
    flow_cube = flow.reshape(3, order, order, order, row_count, columns)
    lower_cube = lower.reshape(number, order, order, 1, columns)
    upper_cube = upper.reshape(number, order, order, 1, columns)
    layer_index = lax.iota(jnp.int32, columns) % CZ
    x_outside_low = jnp.concatenate([lower_cube, nodal_cube[:, far_node, :, :, :-1, :]], axis=3)
    x_low = upwind(nodal_cube[:, 0], x_outside_low, -flow_cube[0, 0], lift)
    x_outside_high = jnp.concatenate([nodal_cube[:, 0, :, :, 1:, :], upper_cube], axis=3)
    x_high = upwind(nodal_cube[:, far_node], x_outside_high, flow_cube[0, far_node], lift)
    y_low = upwind(
        nodal_cube[:, :, 0],
        shift_columns(nodal_cube[:, :, far_node], CZ),
        -flow_cube[1, :, 0],
        lift,
    )
    y_high = upwind(
        nodal_cube[:, :, far_node],
        shift_columns(nodal_cube[:, :, 0], -CZ),
        flow_cube[1, :, far_node],
        lift,
    )
    z_outside_low = jnp.where(
        layer_index == 0, 0.0, shift_columns(nodal_cube[:, :, :, far_node], 1)
    )
    z_low = upwind(nodal_cube[:, :, :, 0], z_outside_low, -flow_cube[2, :, :, 0], lift)
    z_outside_high = jnp.where(
        layer_index == CZ - 1, 0.0, shift_columns(nodal_cube[:, :, :, 0], -1)
    )
    z_high = upwind(
        nodal_cube[:, :, :, far_node], z_outside_high, flow_cube[2, :, :, far_node], lift
    )
    total = result.reshape(number, order, order, order, row_count, columns)
    total = total.at[:, 0].add(x_low).at[:, far_node].add(x_high)
    total = total.at[:, :, 0].add(y_low).at[:, :, far_node].add(y_high)
    total = total.at[:, :, :, 0].add(z_low).at[:, :, :, far_node].add(z_high)
    return total.reshape(number, nodes, row_count, columns)


def face_pair(fields, order):
    number = fields.shape[0]
    row_count = fields.shape[2]
    columns = fields.shape[3]
    nodal_cube = fields.reshape(number, order, order * order, row_count, columns)
    return jnp.stack(
        [nodal_cube[:, 0, :, 0, :], nodal_cube[:, order - 1, :, row_count - 1, :]], axis=2
    )


def fine_operate(fields, flow, gradient):
    widened = extended(face_pair(fields, 4), (("space", 2),), 1)
    return apply_operator(fields, flow, gradient, 4, fine_lift, widened[:, :, 0], widened[:, :, 3])


def coarse_operate(fields, flow_coarse, gradient):
    widened = extended(face_pair(fields, 2), (("space", 2),), 1)
    return apply_operator(
        fields, flow_coarse, gradient, 2, coarse_lift, widened[:, :, 0], widened[:, :, 3]
    )


def fine_sweeps(states, slice_begin, fine_apply):
    evaluated = fine_apply(jnp.concatenate([states, slice_begin[None]], axis=0))
    previous = evaluated[:3]
    begin_rate = evaluated[3]
    half_step = 0.5 * slice_step
    middle = slice_begin
    closing = slice_begin
    for sweep_index in range(SWEEPS):
        middle = (
            slice_begin
            + half_step * (begin_rate - previous[0])
            + slice_step * (5.0 * previous[0] + 8.0 * previous[1] - previous[2]) / 24.0
        )
        middle_rate = fine_apply(middle[None])[0]
        closing = (
            middle
            + half_step * (middle_rate - previous[1])
            + slice_step * (8.0 * previous[1] + 5.0 * previous[2] - previous[0]) / 24.0
        )
        closing_rate = fine_apply(closing[None])[0]
        previous = jnp.stack([begin_rate, middle_rate, closing_rate])
    return (middle, closing, previous)


def coarse_terms(slice_begin, closing, rates, restrict_cube, coarse_apply):
    quadrature = slice_step * (rates[0] + 4.0 * rates[1] + rates[2]) / 6.0
    restricted = jnp.einsum(
        "kn,fnxe->fkxe",
        restrict_cube,
        jnp.stack([slice_begin, closing, quadrature]),
        precision=highest,
    )
    coarse_old = restricted[:2]
    coarse_rates = coarse_apply(coarse_old)
    tau_term = restricted[2] - 0.5 * slice_step * (coarse_rates[0] + coarse_rates[1])
    offset = (
        -slice_step * coarse_rates[0]
        + 0.5 * slice_step * (coarse_rates[0] + coarse_rates[1])
        + tau_term
    )
    return (coarse_old, offset)


def corrected(slice_begin, middle, closing, coarse_old, chain_begin, finish, prolong_cube):
    delta_begin = chain_begin - coarse_old[0]
    delta_end = finish - coarse_old[1]
    deltas = jnp.stack([delta_begin, 0.5 * (delta_begin + delta_end), delta_end])
    lifted = jnp.einsum("nk,fkxe->fnxe", prolong_cube, deltas, precision=highest)
    return jnp.stack([slice_begin, middle, closing]) + lifted


def body(node_states, initial_state, velocity):
    gradient_fine, gradient_coarse, restrict_cube, prolong_cube = level_tables()
    flow = velocity.astype(jnp.float32)
    flow_coarse = corner_values(flow)
    is_first = lax.axis_index("tm") == 0
    states = node_states[0]
    arrived = passed_along(states[2], "tm", 1)
    slice_begin = jnp.where(is_first, initial_state, arrived)

    def fine_apply(fields):
        return fine_operate(fields, flow, gradient_fine)

    def coarse_apply(fields):
        return coarse_operate(fields, flow_coarse, gradient_coarse)

    middle, closing, rates = fine_sweeps(states, slice_begin, fine_apply)
    coarse_old, offset = coarse_terms(slice_begin, closing, rates, restrict_cube, coarse_apply)
    chain_start = jnp.einsum("kn,nxe->kxe", restrict_cube, initial_state, precision=highest)

    def evolve(values):
        return values + slice_step * coarse_apply(values[None])[0]

    slices = lax.axis_size("tm")

    def advance(step_index, carry):
        arrived_end = passed_along(evolve(carry) + offset, "tm", 1)
        return jnp.where(is_first, chain_start, arrived_end)

    chain_begin = lax.fori_loop(0, slices - 1, advance, chain_start)
    finish = evolve(chain_begin) + offset
    return corrected(slice_begin, middle, closing, coarse_old, chain_begin, finish, prolong_cube)[
        None
    ]


def solution(mesh):
    return jax.shard_map(
        body,
        mesh=mesh,
        in_specs=(
            P("tm", None, None, "space", None),
            P(None, "space", None),
            P(None, None, "space", None),
        ),
        out_specs=P("tm", None, None, "space", None),
        check_vma=False,
    )
```

profile of v0, /device:TPU:95, one launch (start us, length us, event | category | flops | bytes accessed | tf_op | source)
XLA Modules:
  0.0 429.2 jit_solution(16316821310985903603)
XLA Ops:
  1.1 8.8 %collective-permute-start.3 = (f32[64,4,128]{2,0,1:T(8,128)S(1)}, f32[64,4,128]{2,0,1:T(8,128)S(1)}, u32[]{:S(2)}, u32[]{:S(2)}) collective-permute-start(f32[64,4,128]{2,0,1:T(8,128)S(1)} %slice_bitcast_fusion.32), channel_id=1, source_target_pairs={{0,32},{32,64},{64,96},{96,128},{128,160},{160,192},{192,224},{224... | collective-permute-start | bytes 393224 | tf_op jit(solution)/shard_map/ppermute | solution.py:33
  14.4 7.8 %collective-permute-done.3 = f32[64,4,128]{2,0,1:T(8,128)S(1)} collective-permute-done((f32[64,4,128]{2,0,1:T(8,128)S(1)}, f32[64,4,128]{2,0,1:T(8,128)S(1)}, u32[]{:S(2)}, u32[]{:S(2)}) %collective-permute-start.3) | collective-permute-done | bytes 131104 | tf_op jit(solution)/shard_map/ppermute | solution.py:33
  24.2 5.1 %collective-permute-start.4 = (f32[4,16,1,128]{3,1,0,2:T(8,128)S(1)}, f32[4,16,1,128]{3,1,0,2:T(8,128)S(1)}, u32[]{:S(2)}, u32[]{:S(2)}) collective-permute-start(f32[4,16,1,128]{3,1,0,2:T(8,128)S(1)} %get-tuple-element.1013), channel_id=1, source_target_pairs={{0,1},{1,2},{2,3},{3,4},{4,5},{5,6},{6,7},{7,8},{8,9},{9,10},{10,1... | collective-permute-start | bytes 98312 | tf_op jit(solution)/shard_map/ppermute | solution.py:24
  31.7 5.1 %collective-permute-done.5 = f32[4,16,1,128]{3,1,0,2:T(8,128)S(1)} collective-permute-done((f32[4,16,1,128]{3,1,0,2:T(8,128)S(1)}, f32[4,16,1,128]{3,1,0,2:T(8,128)S(1)}, u32[]{:S(2)}, u32[]{:S(2)}) %collective-permute-start.5) | collective-permute-done | bytes 32800 | tf_op jit(solution)/shard_map/ppermute | solution.py:25
  119.5 297.3 %while.74 = (s32[]{:T(128)}, f32[8,4,128]{2,0,1:T(8,128)S(1)}, pred[]{:T(512)}, f32[3,8,4,128]{3,1,2,0:T(8,128)S(1)}, f32[1,2,2,4,128]{4,2,1,3,0:T(2,128)S(1)}, ...) while((s32[]{:T(128)}, f32[8,4,128]{2,0,1:T(8,128)S(1)}, ...), condition=%wide.region_1.2_spmd.clone, body=%wide.region_0.1_spmd.sunk.clone.sunk | while | flops 1278978 | bytes 957694 | solution.py:257
  129.0 4.9 %collective-permute-start.2 = (f32[8,4,128]{2,0,1:T(8,128)S(1)}, f32[8,4,128]{2,0,1:T(8,128)S(1)}, u32[]{:S(2)}, u32[]{:S(2)}) collective-permute-start(f32[8,4,128]{2,0,1:T(8,128)S(1)} %add_add_fusion.2), channel_id=1, source_target_pairs={{0,32},{32,64},{64,96},{96,128},{128,160},{160,192},{192,224},{224... | collective-permute-start | bytes 49160 | tf_op jit(solution)/shard_map/while/body/eval_jaxpr/ppermute | solution.py:33
  143.8 4.6 %collective-permute-done.1 = f32[1,4,1,128]{3,1,2,0:T(4,128)S(1)} collective-permute-done((f32[1,4,1,128]{3,1,2,0:T(4,128)S(1)}, f32[1,4,1,128]{3,1,2,0:T(4,128)S(1)}, u32[]{:S(2)}, u32[]{:S(2)}) %collective-permute-start.1) | collective-permute-done | bytes 2080 | tf_op jit(solution)/shard_map/while/body/eval_jaxpr/ppermute | solution.py:25
  152.8 5.3 %collective-permute-done.2 = f32[8,4,128]{2,0,1:T(8,128)S(1)} collective-permute-done((f32[8,4,128]{2,0,1:T(8,128)S(1)}, f32[8,4,128]{2,0,1:T(8,128)S(1)}, u32[]{:S(2)}, u32[]{:S(2)}) %collective-permute-start.2) | collective-permute-done | bytes 16416 | tf_op jit(solution)/shard_map/while/body/eval_jaxpr/ppermute | solution.py:33
  163.7 4.6 %collective-permute-done.1 = f32[1,4,1,128]{3,1,2,0:T(4,128)S(1)} collective-permute-done((f32[1,4,1,128]{3,1,2,0:T(4,128)S(1)}, f32[1,4,1,128]{3,1,2,0:T(4,128)S(1)}, u32[]{:S(2)}, u32[]{:S(2)}) %collective-permute-start.1) | collective-permute-done | bytes 2080 | tf_op jit(solution)/shard_map/while/body/eval_jaxpr/ppermute | solution.py:25
  171.8 6.2 %collective-permute-done.2 = f32[8,4,128]{2,0,1:T(8,128)S(1)} collective-permute-done((f32[8,4,128]{2,0,1:T(8,128)S(1)}, f32[8,4,128]{2,0,1:T(8,128)S(1)}, u32[]{:S(2)}, u32[]{:S(2)}) %collective-permute-start.2) | collective-permute-done | bytes 16416 | tf_op jit(solution)/shard_map/while/body/eval_jaxpr/ppermute | solution.py:33
  190.8 7.1 %collective-permute-done.2 = f32[8,4,128]{2,0,1:T(8,128)S(1)} collective-permute-done((f32[8,4,128]{2,0,1:T(8,128)S(1)}, f32[8,4,128]{2,0,1:T(8,128)S(1)}, u32[]{:S(2)}, u32[]{:S(2)}) %collective-permute-start.2) | collective-permute-done | bytes 16416 | tf_op jit(solution)/shard_map/while/body/eval_jaxpr/ppermute | solution.py:33
  210.5 7.4 %collective-permute-done.2 = f32[8,4,128]{2,0,1:T(8,128)S(1)} collective-permute-done((f32[8,4,128]{2,0,1:T(8,128)S(1)}, f32[8,4,128]{2,0,1:T(8,128)S(1)}, u32[]{:S(2)}, u32[]{:S(2)}) %collective-permute-start.2) | collective-permute-done | bytes 16416 | tf_op jit(solution)/shard_map/while/body/eval_jaxpr/ppermute | solution.py:33
  230.3 7.4 %collective-permute-done.2 = f32[8,4,128]{2,0,1:T(8,128)S(1)} collective-permute-done((f32[8,4,128]{2,0,1:T(8,128)S(1)}, f32[8,4,128]{2,0,1:T(8,128)S(1)}, u32[]{:S(2)}, u32[]{:S(2)}) %collective-permute-start.2) | collective-permute-done | bytes 16416 | tf_op jit(solution)/shard_map/while/body/eval_jaxpr/ppermute | solution.py:33
  250.2 7.4 %collective-permute-done.2 = f32[8,4,128]{2,0,1:T(8,128)S(1)} collective-permute-done((f32[8,4,128]{2,0,1:T(8,128)S(1)}, f32[8,4,128]{2,0,1:T(8,128)S(1)}, u32[]{:S(2)}, u32[]{:S(2)}) %collective-permute-start.2) | collective-permute-done | bytes 16416 | tf_op jit(solution)/shard_map/while/body/eval_jaxpr/ppermute | solution.py:33
  270.1 7.4 %collective-permute-done.2 = f32[8,4,128]{2,0,1:T(8,128)S(1)} collective-permute-done((f32[8,4,128]{2,0,1:T(8,128)S(1)}, f32[8,4,128]{2,0,1:T(8,128)S(1)}, u32[]{:S(2)}, u32[]{:S(2)}) %collective-permute-start.2) | collective-permute-done | bytes 16416 | tf_op jit(solution)/shard_map/while/body/eval_jaxpr/ppermute | solution.py:33
  290.0 7.4 %collective-permute-done.2 = f32[8,4,128]{2,0,1:T(8,128)S(1)} collective-permute-done((f32[8,4,128]{2,0,1:T(8,128)S(1)}, f32[8,4,128]{2,0,1:T(8,128)S(1)}, u32[]{:S(2)}, u32[]{:S(2)}) %collective-permute-start.2) | collective-permute-done | bytes 16416 | tf_op jit(solution)/shard_map/while/body/eval_jaxpr/ppermute | solution.py:33
  309.9 7.4 %collective-permute-done.2 = f32[8,4,128]{2,0,1:T(8,128)S(1)} collective-permute-done((f32[8,4,128]{2,0,1:T(8,128)S(1)}, f32[8,4,128]{2,0,1:T(8,128)S(1)}, u32[]{:S(2)}, u32[]{:S(2)}) %collective-permute-start.2) | collective-permute-done | bytes 16416 | tf_op jit(solution)/shard_map/while/body/eval_jaxpr/ppermute | solution.py:33
  322.8 4.6 %collective-permute-done.1 = f32[1,4,1,128]{3,1,2,0:T(4,128)S(1)} collective-permute-done((f32[1,4,1,128]{3,1,2,0:T(4,128)S(1)}, f32[1,4,1,128]{3,1,2,0:T(4,128)S(1)}, u32[]{:S(2)}, u32[]{:S(2)}) %collective-permute-start.1) | collective-permute-done | bytes 2080 | tf_op jit(solution)/shard_map/while/body/eval_jaxpr/ppermute | solution.py:25
  329.8 7.4 %collective-permute-done.2 = f32[8,4,128]{2,0,1:T(8,128)S(1)} collective-permute-done((f32[8,4,128]{2,0,1:T(8,128)S(1)}, f32[8,4,128]{2,0,1:T(8,128)S(1)}, u32[]{:S(2)}, u32[]{:S(2)}) %collective-permute-start.2) | collective-permute-done | bytes 16416 | tf_op jit(solution)/shard_map/while/body/eval_jaxpr/ppermute | solution.py:33
  349.7 7.4 %collective-permute-done.2 = f32[8,4,128]{2,0,1:T(8,128)S(1)} collective-permute-done((f32[8,4,128]{2,0,1:T(8,128)S(1)}, f32[8,4,128]{2,0,1:T(8,128)S(1)}, u32[]{:S(2)}, u32[]{:S(2)}) %collective-permute-start.2) | collective-permute-done | bytes 16416 | tf_op jit(solution)/shard_map/while/body/eval_jaxpr/ppermute | solution.py:33
  369.6 7.4 %collective-permute-done.2 = f32[8,4,128]{2,0,1:T(8,128)S(1)} collective-permute-done((f32[8,4,128]{2,0,1:T(8,128)S(1)}, f32[8,4,128]{2,0,1:T(8,128)S(1)}, u32[]{:S(2)}, u32[]{:S(2)}) %collective-permute-start.2) | collective-permute-done | bytes 16416 | tf_op jit(solution)/shard_map/while/body/eval_jaxpr/ppermute | solution.py:33
  389.5 7.4 %collective-permute-done.2 = f32[8,4,128]{2,0,1:T(8,128)S(1)} collective-permute-done((f32[8,4,128]{2,0,1:T(8,128)S(1)}, f32[8,4,128]{2,0,1:T(8,128)S(1)}, u32[]{:S(2)}, u32[]{:S(2)}) %collective-permute-start.2) | collective-permute-done | bytes 16416 | tf_op jit(solution)/shard_map/while/body/eval_jaxpr/ppermute | solution.py:33
  409.4 7.4 %collective-permute-done.2 = f32[8,4,128]{2,0,1:T(8,128)S(1)} collective-permute-done((f32[8,4,128]{2,0,1:T(8,128)S(1)}, f32[8,4,128]{2,0,1:T(8,128)S(1)}, u32[]{:S(2)}, u32[]{:S(2)}) %collective-permute-start.2) | collective-permute-done | bytes 16416 | tf_op jit(solution)/shard_map/while/body/eval_jaxpr/ppermute | solution.py:33
  422.2 5.0 %collective-permute-done.21 = f32[1,4,1,128]{3,1,2,0:T(4,128)S(1)} collective-permute-done((f32[1,4,1,128]{3,1,2,0:T(4,128)S(1)}, f32[1,4,1,128]{3,1,2,0:T(4,128)S(1)}, u32[]{:S(2)}, u32[]{:S(2)}) %collective-permute-start.21) | collective-permute-done | bytes 2080 | tf_op jit(solution)/shard_map/ppermute | solution.py:25
  (772 shorter events, 275.0 us)
Async XLA Ops:
  1.1 21.1 %collective-permute-start.3 = (f32[64,4,128]{2,0,1:T(8,128)S(1)}, f32[64,4,128]{2,0,1:T(8,128)S(1)}, u32[]{:S(2)}, u32[]{:S(2)}) collective-permute-start(f32[64,4,128]{2,0,1:T(8,128)S(1)} %slice_bitcast_fusion.32), channel_id=1, source_target_pairs={{0,32},{32,64},{64,96},{96,128},{128,160},{160,192},{192,224},{224... | collective-permute-start | bytes 393224 | tf_op jit(solution)/shard_map/ppermute | solution.py:33
  24.2 7.4 %collective-permute-start.4 = (f32[4,16,1,128]{3,1,0,2:T(8,128)S(1)}, f32[4,16,1,128]{3,1,0,2:T(8,128)S(1)}, u32[]{:S(2)}, u32[]{:S(2)}) collective-permute-start(f32[4,16,1,128]{3,1,0,2:T(8,128)S(1)} %get-tuple-element.1013), channel_id=1, source_target_pairs={{0,1},{1,2},{2,3},{3,4},{4,5},{5,6},{6,7},{7,8},{8,9},{9,10},{10,1... | collective-permute-start | bytes 98312 | tf_op jit(solution)/shard_map/ppermute | solution.py:24
  29.5 7.3 %collective-permute-start.5 = (f32[4,16,1,128]{3,1,0,2:T(8,128)S(1)}, f32[4,16,1,128]{3,1,0,2:T(8,128)S(1)}, u32[]{:S(2)}, u32[]{:S(2)}) collective-permute-start(f32[4,16,1,128]{3,1,0,2:T(8,128)S(1)} %get-tuple-element.1012), channel_id=1, source_target_pairs={{1,0},{2,1},{3,2},{4,3},{5,4},{6,5},{7,6},{8,7},{9,8},{10,9},{11,1... | collective-permute-start | bytes 98312 | tf_op jit(solution)/shard_map/ppermute | solution.py:25
  46.4 7.1 %collective-permute-start.7 = (f32[1,16,1,128]{3,1,2,0:T(8,128)S(1)}, f32[1,16,1,128]{3,1,2,0:T(8,128)S(1)}, u32[]{:S(2)}, u32[]{:S(2)}) collective-permute-start(f32[1,16,1,128]{3,1,2,0:T(8,128)S(1)} %get-tuple-element.1087), channel_id=1, source_target_pairs={{1,0},{2,1},{3,2},{4,3},{5,4},{6,5},{7,6},{8,7},{9,8},{10,9},{11,1... | collective-permute-start | bytes 24584 | tf_op jit(solution)/shard_map/ppermute | solution.py:25
  57.6 7.1 %collective-permute-start.9 = (f32[1,16,1,128]{3,1,2,0:T(8,128)S(1)}, f32[1,16,1,128]{3,1,2,0:T(8,128)S(1)}, u32[]{:S(2)}, u32[]{:S(2)}) collective-permute-start(f32[1,16,1,128]{3,1,2,0:T(8,128)S(1)} %get-tuple-element.1077), channel_id=1, source_target_pairs={{1,0},{2,1},{3,2},{4,3},{5,4},{6,5},{7,6},{8,7},{9,8},{10,9},{11,1... | collective-permute-start | bytes 24584 | tf_op jit(solution)/shard_map/ppermute | solution.py:25
  68.4 7.1 %collective-permute-start.11 = (f32[1,16,1,128]{3,1,2,0:T(8,128)S(1)}, f32[1,16,1,128]{3,1,2,0:T(8,128)S(1)}, u32[]{:S(2)}, u32[]{:S(2)}) collective-permute-start(f32[1,16,1,128]{3,1,2,0:T(8,128)S(1)} %get-tuple-element.1065), channel_id=1, source_target_pairs={{1,0},{2,1},{3,2},{4,3},{5,4},{6,5},{7,6},{8,7},{9,8},{10,9},{11,1... | collective-permute-start | bytes 24584 | tf_op jit(solution)/shard_map/ppermute | solution.py:25
  79.6 7.1 %collective-permute-start.13 = (f32[1,16,1,128]{3,1,2,0:T(8,128)S(1)}, f32[1,16,1,128]{3,1,2,0:T(8,128)S(1)}, u32[]{:S(2)}, u32[]{:S(2)}) collective-permute-start(f32[1,16,1,128]{3,1,2,0:T(8,128)S(1)} %get-tuple-element.1053), channel_id=1, source_target_pairs={{1,0},{2,1},{3,2},{4,3},{5,4},{6,5},{7,6},{8,7},{9,8},{10,9},{11,1... | collective-permute-start | bytes 24584 | tf_op jit(solution)/shard_map/ppermute | solution.py:25
  90.3 7.1 %collective-permute-start.15 = (f32[1,16,1,128]{3,1,2,0:T(8,128)S(1)}, f32[1,16,1,128]{3,1,2,0:T(8,128)S(1)}, u32[]{:S(2)}, u32[]{:S(2)}) collective-permute-start(f32[1,16,1,128]{3,1,2,0:T(8,128)S(1)} %get-tuple-element.1043), channel_id=1, source_target_pairs={{1,0},{2,1},{3,2},{4,3},{5,4},{6,5},{7,6},{8,7},{9,8},{10,9},{11,1... | collective-permute-start | bytes 24584 | tf_op jit(solution)/shard_map/ppermute | solution.py:25
  101.1 7.1 %collective-permute-start.17 = (f32[1,16,1,128]{3,1,2,0:T(8,128)S(1)}, f32[1,16,1,128]{3,1,2,0:T(8,128)S(1)}, u32[]{:S(2)}, u32[]{:S(2)}) collective-permute-start(f32[1,16,1,128]{3,1,2,0:T(8,128)S(1)} %get-tuple-element.1033), channel_id=1, source_target_pairs={{1,0},{2,1},{3,2},{4,3},{5,4},{6,5},{7,6},{8,7},{9,8},{10,9},{11,1... | collective-permute-start | bytes 24584 | tf_op jit(solution)/shard_map/ppermute | solution.py:25
  129.0 9.3 %collective-permute-start.2 = (f32[8,4,128]{2,0,1:T(8,128)S(1)}, f32[8,4,128]{2,0,1:T(8,128)S(1)}, u32[]{:S(2)}, u32[]{:S(2)}) collective-permute-start(f32[8,4,128]{2,0,1:T(8,128)S(1)} %add_add_fusion.2), channel_id=1, source_target_pairs={{0,32},{32,64},{64,96},{96,128},{128,160},{160,192},{192,224},{224... | collective-permute-start | bytes 49160 | tf_op jit(solution)/shard_map/while/body/eval_jaxpr/ppermute | solution.py:33
  148.8 9.3 %collective-permute-start.2 = (f32[8,4,128]{2,0,1:T(8,128)S(1)}, f32[8,4,128]{2,0,1:T(8,128)S(1)}, u32[]{:S(2)}, u32[]{:S(2)}) collective-permute-start(f32[8,4,128]{2,0,1:T(8,128)S(1)} %add_add_fusion.2), channel_id=1, source_target_pairs={{0,32},{32,64},{64,96},{96,128},{128,160},{160,192},{192,224},{224... | collective-permute-start | bytes 49160 | tf_op jit(solution)/shard_map/while/body/eval_jaxpr/ppermute | solution.py:33
  168.7 9.3 %collective-permute-start.2 = (f32[8,4,128]{2,0,1:T(8,128)S(1)}, f32[8,4,128]{2,0,1:T(8,128)S(1)}, u32[]{:S(2)}, u32[]{:S(2)}) collective-permute-start(f32[8,4,128]{2,0,1:T(8,128)S(1)} %add_add_fusion.2), channel_id=1, source_target_pairs={{0,32},{32,64},{64,96},{96,128},{128,160},{160,192},{192,224},{224... | collective-permute-start | bytes 49160 | tf_op jit(solution)/shard_map/while/body/eval_jaxpr/ppermute | solution.py:33
  188.6 9.3 %collective-permute-start.2 = (f32[8,4,128]{2,0,1:T(8,128)S(1)}, f32[8,4,128]{2,0,1:T(8,128)S(1)}, u32[]{:S(2)}, u32[]{:S(2)}) collective-permute-start(f32[8,4,128]{2,0,1:T(8,128)S(1)} %add_add_fusion.2), channel_id=1, source_target_pairs={{0,32},{32,64},{64,96},{96,128},{128,160},{160,192},{192,224},{224... | collective-permute-start | bytes 49160 | tf_op jit(solution)/shard_map/while/body/eval_jaxpr/ppermute | solution.py:33
  208.5 9.3 %collective-permute-start.2 = (f32[8,4,128]{2,0,1:T(8,128)S(1)}, f32[8,4,128]{2,0,1:T(8,128)S(1)}, u32[]{:S(2)}, u32[]{:S(2)}) collective-permute-start(f32[8,4,128]{2,0,1:T(8,128)S(1)} %add_add_fusion.2), channel_id=1, source_target_pairs={{0,32},{32,64},{64,96},{96,128},{128,160},{160,192},{192,224},{224... | collective-permute-start | bytes 49160 | tf_op jit(solution)/shard_map/while/body/eval_jaxpr/ppermute | solution.py:33
  228.4 9.3 %collective-permute-start.2 = (f32[8,4,128]{2,0,1:T(8,128)S(1)}, f32[8,4,128]{2,0,1:T(8,128)S(1)}, u32[]{:S(2)}, u32[]{:S(2)}) collective-permute-start(f32[8,4,128]{2,0,1:T(8,128)S(1)} %add_add_fusion.2), channel_id=1, source_target_pairs={{0,32},{32,64},{64,96},{96,128},{128,160},{160,192},{192,224},{224... | collective-permute-start | bytes 49160 | tf_op jit(solution)/shard_map/while/body/eval_jaxpr/ppermute | solution.py:33
  248.3 9.3 %collective-permute-start.2 = (f32[8,4,128]{2,0,1:T(8,128)S(1)}, f32[8,4,128]{2,0,1:T(8,128)S(1)}, u32[]{:S(2)}, u32[]{:S(2)}) collective-permute-start(f32[8,4,128]{2,0,1:T(8,128)S(1)} %add_add_fusion.2), channel_id=1, source_target_pairs={{0,32},{32,64},{64,96},{96,128},{128,160},{160,192},{192,224},{224... | collective-permute-start | bytes 49160 | tf_op jit(solution)/shard_map/while/body/eval_jaxpr/ppermute | solution.py:33
  268.2 9.3 %collective-permute-start.2 = (f32[8,4,128]{2,0,1:T(8,128)S(1)}, f32[8,4,128]{2,0,1:T(8,128)S(1)}, u32[]{:S(2)}, u32[]{:S(2)}) collective-permute-start(f32[8,4,128]{2,0,1:T(8,128)S(1)} %add_add_fusion.2), channel_id=1, source_target_pairs={{0,32},{32,64},{64,96},{96,128},{128,160},{160,192},{192,224},{224... | collective-permute-start | bytes 49160 | tf_op jit(solution)/shard_map/while/body/eval_jaxpr/ppermute | solution.py:33
  288.1 9.3 %collective-permute-start.2 = (f32[8,4,128]{2,0,1:T(8,128)S(1)}, f32[8,4,128]{2,0,1:T(8,128)S(1)}, u32[]{:S(2)}, u32[]{:S(2)}) collective-permute-start(f32[8,4,128]{2,0,1:T(8,128)S(1)} %add_add_fusion.2), channel_id=1, source_target_pairs={{0,32},{32,64},{64,96},{96,128},{128,160},{160,192},{192,224},{224... | collective-permute-start | bytes 49160 | tf_op jit(solution)/shard_map/while/body/eval_jaxpr/ppermute | solution.py:33
  308.0 9.3 %collective-permute-start.2 = (f32[8,4,128]{2,0,1:T(8,128)S(1)}, f32[8,4,128]{2,0,1:T(8,128)S(1)}, u32[]{:S(2)}, u32[]{:S(2)}) collective-permute-start(f32[8,4,128]{2,0,1:T(8,128)S(1)} %add_add_fusion.2), channel_id=1, source_target_pairs={{0,32},{32,64},{64,96},{96,128},{128,160},{160,192},{192,224},{224... | collective-permute-start | bytes 49160 | tf_op jit(solution)/shard_map/while/body/eval_jaxpr/ppermute | solution.py:33
  327.9 9.3 %collective-permute-start.2 = (f32[8,4,128]{2,0,1:T(8,128)S(1)}, f32[8,4,128]{2,0,1:T(8,128)S(1)}, u32[]{:S(2)}, u32[]{:S(2)}) collective-permute-start(f32[8,4,128]{2,0,1:T(8,128)S(1)} %add_add_fusion.2), channel_id=1, source_target_pairs={{0,32},{32,64},{64,96},{96,128},{128,160},{160,192},{192,224},{224... | collective-permute-start | bytes 49160 | tf_op jit(solution)/shard_map/while/body/eval_jaxpr/ppermute | solution.py:33
  347.8 9.3 %collective-permute-start.2 = (f32[8,4,128]{2,0,1:T(8,128)S(1)}, f32[8,4,128]{2,0,1:T(8,128)S(1)}, u32[]{:S(2)}, u32[]{:S(2)}) collective-permute-start(f32[8,4,128]{2,0,1:T(8,128)S(1)} %add_add_fusion.2), channel_id=1, source_target_pairs={{0,32},{32,64},{64,96},{96,128},{128,160},{160,192},{192,224},{224... | collective-permute-start | bytes 49160 | tf_op jit(solution)/shard_map/while/body/eval_jaxpr/ppermute | solution.py:33
  367.7 9.3 %collective-permute-start.2 = (f32[8,4,128]{2,0,1:T(8,128)S(1)}, f32[8,4,128]{2,0,1:T(8,128)S(1)}, u32[]{:S(2)}, u32[]{:S(2)}) collective-permute-start(f32[8,4,128]{2,0,1:T(8,128)S(1)} %add_add_fusion.2), channel_id=1, source_target_pairs={{0,32},{32,64},{64,96},{96,128},{128,160},{160,192},{192,224},{224... | collective-permute-start | bytes 49160 | tf_op jit(solution)/shard_map/while/body/eval_jaxpr/ppermute | solution.py:33
  387.6 9.3 %collective-permute-start.2 = (f32[8,4,128]{2,0,1:T(8,128)S(1)}, f32[8,4,128]{2,0,1:T(8,128)S(1)}, u32[]{:S(2)}, u32[]{:S(2)}) collective-permute-start(f32[8,4,128]{2,0,1:T(8,128)S(1)} %add_add_fusion.2), channel_id=1, source_target_pairs={{0,32},{32,64},{64,96},{96,128},{128,160},{160,192},{192,224},{224... | collective-permute-start | bytes 49160 | tf_op jit(solution)/shard_map/while/body/eval_jaxpr/ppermute | solution.py:33
  407.4 9.3 %collective-permute-start.2 = (f32[8,4,128]{2,0,1:T(8,128)S(1)}, f32[8,4,128]{2,0,1:T(8,128)S(1)}, u32[]{:S(2)}, u32[]{:S(2)}) collective-permute-start(f32[8,4,128]{2,0,1:T(8,128)S(1)} %add_add_fusion.2), channel_id=1, source_target_pairs={{0,32},{32,64},{64,96},{96,128},{128,160},{160,192},{192,224},{224... | collective-permute-start | bytes 49160 | tf_op jit(solution)/shard_map/while/body/eval_jaxpr/ppermute | solution.py:33
  (50 other events, 904.2 us)
where the time goes:
time: 433 us; the launch traced here: 429 us
  waiting for transfers between devices  220 us (51%)
  starting transfers between devices  161 us (37%)
  local copies, waits for them, and re-layouts  22.4 us (5%)
  other arithmetic  11.6 us (3%)
  matrix products  9.64 us (2%)
    ppermute x16, waiting for transfers between devices, passed_along(): return lax.ppermute(block, axis, route)  112 us
    ppermute x24, waiting for transfers between devices, extended(): after = lax.ppermute(initial, axis, down)  109 us
    ppermute x24, starting transfers between devices, extended(): before = lax.ppermute(last, axis, up)  67 us
    ppermute x24, starting transfers between devices, extended(): after = lax.ppermute(initial, axis, down)  49.8 us
    ppermute x16, starting transfers between devices, passed_along(): return lax.ppermute(block, axis, route)  44.1 us
  transfers between devices with their start and end apart: 64, of which 40 were waited for; matrix products, arithmetic and copies ran while one was open for 3% of the time, Pallas kernels for 0%

commit v1 on v0

v1 whole, which is shorter than its diff:
```python
import functools

import jax
import jax.numpy as jnp
import numpy as np
from jax import lax
from jax.experimental import pallas as pl
from jax.experimental.pallas import tpu as pltpu
from jax.sharding import PartitionSpec as P

MESH = pl.DeviceIdType.MESH
CZ = 16
LANES = 128
GROUP = 4
H = 0.08
DT = 0.5 * H
LIFT = 6.0
ROWS = 4
REACH = 3
SPAN = (2 * REACH + 1) * ROWS
MID = REACH * ROWS
FIELD = (4, 4, 2, 8, LANES)


def lagrange_derivative(points):
    number = len(points)
    weights = np.array(
        [1.0 / np.prod([points[i] - points[j] for j in range(number) if j != i]) for i in range(number)]
    )
    derivative = np.zeros((number, number))
    for i in range(number):
        for j in range(number):
            if i != j:
                derivative[i, j] = weights[j] / weights[i] / (points[i] - points[j])
        derivative[i, i] = -np.sum(derivative[i])
    return derivative


POINTS = np.array([-1.0, -1.0 / np.sqrt(5.0), 1.0 / np.sqrt(5.0), 1.0])
WEIGHTS = np.array([1.0, 5.0, 5.0, 1.0]) / 6.0
DER = lagrange_derivative(POINTS)
PRO = np.stack([(1.0 - POINTS) / 2.0, (1.0 + POINTS) / 2.0], axis=1)
RES = PRO.T * WEIGHTS[None, :]


def weighted(terms):
    total = None
    for factor, value in terms:
        factor = float(factor)
        if abs(factor) < 1e-12:
            continue
        piece = value if factor == 1.0 else factor * value
        total = piece if total is None else total + piece
    return total


def kernel(
    steps,
    columns,
    states_hbm,
    start_hbm,
    wind_hbm,
    out_hbm,
    states,
    wind,
    begin,
    nv,
    diag,
    xli,
    xhi,
    xlh,
    xhh,
    yl,
    yh,
    zl,
    zh,
    rates,
    first_rate,
    mid_state,
    end_state,
    base,
    send,
    recv,
    shuffle,
    flows,
    coef,
    old0,
    old1,
    group,
    partial,
    near,
    mid,
    far,
    result,
    load_sem,
    store_sem,
    fine_send,
    fine_recv,
    begin_send,
    begin_recv,
    flow_send,
    flow_recv,
    row_send,
    row_recv,
    group_send,
    group_recv,
    side_send,
    side_recv,
    part_send,
    part_recv,
):
    n = lax.axis_index("tm")
    s = lax.axis_index("space")
    g = n // GROUP
    z = n % GROUP
    groups = steps // GROUP

    sub = lax.broadcasted_iota(jnp.int32, (8, LANES), 0)
    lane = lax.broadcasted_iota(jnp.int32, (8, LANES), 1)
    parity = sub // 4
    row = sub % 4

    def split(even, odd):
        return jnp.where(parity == 0, jnp.float32(even), jnp.float32(odd))

    def remote(src, dst, ssem, rsem, device):
        return pltpu.make_async_remote_copy(
            src_ref=src, dst_ref=dst, send_sem=ssem, recv_sem=rsem, device_id=device, device_id_type=MESH
        )

    has = {-1: s > 0, 1: s < columns - 1}

    def inside(d):
        if d == 0:
            return None
        return s + d >= 0 if d < 0 else s + d < columns

    def both(a, b):
        if a is None:
            return b
        if b is None:
            return a
        return jnp.logical_and(a, b)

    def when(cond, run):
        if cond is None:
            run()
        else:
            pl.when(cond)(run)

    transfers = {}

    def add(name, sends, receives, make, partner):
        transfers.setdefault(name, []).append((sends, receives, make, partner))

    for k, d in enumerate((-1, 1)):
        add(
            "states",
            has[d],
            has[-d],
            functools.partial(
                remote,
                send.at[k, pl.ds(0, 3)],
                recv.at[1 - k, pl.ds(0, 3)],
                fine_send.at[k, 0],
                fine_recv.at[1 - k, 0],
                (n, s + d),
            ),
            None,
        )
        add(
            "begin_trace",
            both(n < steps - 1, has[d]),
            both(n > 0, has[-d]),
            functools.partial(
                remote,
                send.at[k, 2],
                recv.at[1 - k, 3],
                fine_send.at[k, 1],
                fine_recv.at[1 - k, 1],
                (n + 1, s + d),
            ),
            (n - 1, s - d),
        )
        add(
            "first_trace",
            both(n == 0, has[d]),
            both(n == 0, has[-d]),
            functools.partial(
                remote,
                send.at[k, 3],
                recv.at[1 - k, 3],
                fine_send.at[k, 2],
                fine_recv.at[1 - k, 1],
                (n, s + d),
            ),
            None,
        )
        for index, buffer in enumerate((old0, old1)):
            add(
                f"row{index}",
                has[d],
                has[-d],
                functools.partial(
                    remote,
                    buffer.at[1 if d < 0 else ROWS],
                    buffer.at[ROWS + 1 if d < 0 else 0],
                    row_send.at[k, index],
                    row_recv.at[1 - k, index],
                    (n, s + d),
                ),
                None,
            )
        add(
            "side",
            has[d],
            has[-d],
            functools.partial(
                remote,
                group.at[:, pl.ds(ROWS, ROWS)],
                group.at[:, pl.ds(2 * ROWS if d < 0 else 0, ROWS)],
                side_send.at[k],
                side_recv.at[1 - k],
                (n, s + d),
            ),
            None,
        )
    add(
        "begin",
        n < steps - 1,
        n > 0,
        functools.partial(remote, states_hbm.at[2], begin, begin_send, begin_recv, (n + 1, s)),
        (n - 1, s),
    )
    for index, d in enumerate((-3, -2, -1, 1, 2, 3)):
        add(
            "flow",
            inside(d),
            inside(-d),
            functools.partial(
                remote,
                flows.at[REACH],
                flows.at[REACH - d],
                flow_send.at[index],
                flow_recv.at[index],
                (n, s + d),
            ),
            (n, s - d),
        )
    for shift in (1, 2, 3):
        add(
            "group",
            None,
            None,
            functools.partial(
                remote,
                group.at[z, pl.ds(ROWS, ROWS)],
                group.at[z, pl.ds(ROWS, ROWS)],
                group_send.at[shift - 1],
                group_recv.at[shift - 1],
                (g * GROUP + (z + shift) % GROUP, s),
            ),
            (g * GROUP + (z + GROUP - shift) % GROUP, s),
        )
    slot = 0
    for distance, buffer in ((1, near), (2, mid), (3, far)):
        for d in range(-distance, distance + 1):
            add(
                "part",
                both(g + distance < groups, inside(d)),
                both(g >= distance, inside(-d)),
                functools.partial(
                    remote,
                    partial,
                    buffer.at[pl.ds((distance - d) * ROWS, ROWS)],
                    part_send.at[slot],
                    part_recv.at[slot],
                    (n + distance * GROUP, s + d),
                ),
                (n - distance * GROUP, s - d),
            )
            slot += 1

    def start(name):
        for sends, _, make, _ in transfers[name]:
            when(sends, lambda make=make: make().start())

    def arrive(name):
        for _, receives, make, _ in transfers[name]:
            when(receives, lambda make=make: make().wait_recv())

    def sent(name):
        for sends, _, make, _ in transfers[name]:
            when(sends, lambda make=make: make().wait_send())

    load_states = pltpu.make_async_copy(states_hbm, states, load_sem.at[0])
    load_wind = pltpu.make_async_copy(wind_hbm, wind, load_sem.at[1])
    load_first = pltpu.make_async_copy(start_hbm, begin, load_sem.at[2])
    load_states.start()
    load_wind.start()
    pl.when(n == 0)(load_first.start)

    recv[...] = jnp.zeros(recv.shape, jnp.float32)
    flows[...] = jnp.zeros(flows.shape, jnp.float32)
    old0[...] = jnp.zeros(old0.shape, jnp.float32)
    old1[...] = jnp.zeros(old1.shape, jnp.float32)
    group[...] = jnp.zeros(group.shape, jnp.float32)
    near[...] = jnp.zeros(near.shape, jnp.float32)
    mid[...] = jnp.zeros(mid.shape, jnp.float32)
    far[...] = jnp.zeros(far.shape, jnp.float32)

    barrier = pltpu.get_barrier_semaphore()
    expected = jnp.int32(0)

    def greet(cond, device):
        when(
            cond,
            lambda: pl.semaphore_signal(barrier, inc=1, device_id=device, device_id_type=MESH),
        )

    for d in (-1, 1):
        greet(has[d], (n, s + d))
        expected = expected + has[d].astype(jnp.int32)
    for name in ("begin_trace", "begin", "flow", "group", "part"):
        for index, (sends, receives, _, partner) in enumerate(transfers[name]):
            if name == "flow" and index in (2, 3):
                continue
            greet(receives, partner)
            expected = expected + (1 if sends is None else sends.astype(jnp.int32))

    load_states.wait()

    def pack(lower, upper, k_slot):
        for half in range(2):
            low = None
            high = None
            for r in range(4):
                b, hh = (4 * half + r) // 2, r % 2
                lv = lower[b, hh]
                hv = upper[b, hh]
                lv = pltpu.roll(lv, r, 0) if r else lv
                hv = pltpu.roll(hv, (r + 5) % 8, 0) if r != 3 else hv
                low = lv if low is None else jnp.where(row == r, lv, low)
                high = hv if high is None else jnp.where(row == r, hv, high)
            send[0, k_slot, half] = low
            send[1, k_slot, half] = high

    def unpack(k_slot):
        lows, highs = [], []
        for t in range(8):
            half, r = t // 4, t % 4
            lv = recv[0, k_slot, half]
            hv = recv[1, k_slot, half]
            lows.append(pltpu.roll(lv, 8 - r, 0) if r else lv)
            highs.append(pltpu.roll(hv, 3 - r, 0) if r != 3 else hv)
        return (
            jnp.stack(lows).reshape(4, 2, 8, LANES),
            jnp.stack(highs).reshape(4, 2, 8, LANES),
        )

    for k in range(3):
        pack(states[k, 0], states[k, 3], k)

    @pl.when(n == 0)
    def _():
        load_first.wait()
        pack(begin[0], begin[3], 3)

    pl.semaphore_wait(barrier, expected)
    start("begin_trace")
    start("first_trace")
    start("begin")
    start("states")

    load_wind.wait()
    for axis in range(3):
        nv[axis] = -wind[axis].astype(jnp.float32).reshape(FIELD)

    for axis in range(3):
        for i in range(2):
            for j in range(2):
                corner = jnp.where(parity == 0, nv[axis, 3 * i, 3 * j, 0], nv[axis, 3 * i, 3 * j, 1])
                shuffle[pl.ds(8 * (2 * i + j), 8)] = corner
        for r in range(ROWS):
            flows[REACH, r, axis] = shuffle[pl.ds(r, 8, stride=4)]
    start("flow")

    cxl = LIFT * jnp.minimum(nv[0, 0], 0.0)
    cxh = LIFT * jnp.minimum(-nv[0, 3], 0.0)
    xli[...] = jnp.where(row > 0, -cxl, 0.0)
    xlh[...] = jnp.where(row == 0, -cxl, 0.0)
    xhi[...] = jnp.where(row < 3, -cxh, 0.0)
    xhh[...] = jnp.where(row == 3, -cxh, 0.0)
    cyl = LIFT * jnp.minimum(nv[1, :, 0], 0.0)
    cyh = LIFT * jnp.minimum(-nv[1, :, 3], 0.0)
    yl[...] = jnp.where(lane >= CZ, -cyl, 0.0)
    yh[...] = jnp.where(lane < LANES - CZ, -cyh, 0.0)
    czl = jnp.where(parity == 0, LIFT * jnp.minimum(nv[2, :, :, 0], 0.0), 0.0)
    czh = jnp.where(parity == 1, LIFT * jnp.minimum(-nv[2, :, :, 1], 0.0), 0.0)
    layer = lane % CZ
    zl[...] = jnp.where(layer > 0, -czl, 0.0)
    zh[...] = jnp.where(layer < CZ - 1, -czh, 0.0)
    diag[:, :, 0] = czl
    diag[:, :, 1] = czh
    diag[0] = diag[0] + cxl
    diag[3] = diag[3] + cxh
    diag[:, 0] = diag[:, 0] + cyl
    diag[:, 3] = diag[:, 3] + cyh

    same = [[split(DER[2 * i, 2 * j], DER[2 * i + 1, 2 * j + 1]) for j in range(2)] for i in range(2)]
    cross = [[split(DER[2 * i, 2 * j + 1], DER[2 * i + 1, 2 * j]) for j in range(2)] for i in range(2)]

    def interior(u, out):
        for b in range(4):
            ub = u[:, b]
            turned = pltpu.roll(ub, 4, 2)
            along_x = jnp.stack([weighted([(DER[a, c], ub[c]) for c in range(4)]) for a in range(4)])
            along_y = weighted([(DER[b, c], ub if c == b else u[:, c]) for c in range(4)])
            along_z = jnp.stack(
                [
                    same[i][0] * ub[:, 0]
                    + cross[i][0] * turned[:, 0]
                    + same[i][1] * ub[:, 1]
                    + cross[i][1] * turned[:, 1]
                    for i in range(2)
                ],
                axis=1,
            )
            total = (
                nv[0, :, b] * along_x
                + nv[1, :, b] * along_y
                + nv[2, :, b] * along_z
                + diag[:, b] * ub
            )
            faces = jnp.stack(
                [
                    zl[:, b] * pltpu.roll(turned[:, 1], 1, 2),
                    zh[:, b] * pltpu.roll(turned[:, 0], LANES - 1, 2),
                ],
                axis=1,
            )
            total = total + faces
            if b == 0:
                total = total + yl[...] * pltpu.roll(u[:, 3], CZ, 3)
            if b == 3:
                total = total + yh[...] * pltpu.roll(u[:, 0], LANES - CZ, 3)
            out[0, b] = total[0] + xli[b] * pltpu.roll(ub[3], 1, 1)
            out[1, b] = total[1]
            out[2, b] = total[2]
            out[3, b] = total[3] + xhi[b] * pltpu.roll(ub[0], 7, 1)

    def finish_rate(out, k_slot):
        low, high = unpack(k_slot)
        lower = out[0] + xlh[...] * low
        upper = out[3] + xhh[...] * high
        out[0] = lower
        out[3] = upper
        return lower, upper

    def old_rate(k, carry):
        interior(states.at[k], rates.at[k])
        return carry

    lax.fori_loop(0, 3, old_rate, 0)
    arrive("states")
    for k in range(3):
        finish_rate(rates.at[k], k)

    base[...] = -DT * rates[0] + (H / 24.0) * (5.0 * rates[0] + 8.0 * rates[1] - rates[2])

    arrive("flow")
    top = (sub // 4) % 2 == 0
    middle = (sub // 2) % 2 == 0
    bottom = sub % 2 == 0
    signs = [jnp.where(bit, jnp.float32(-1.0), jnp.float32(1.0)) for bit in (top, middle, bottom)]
    open_y = jnp.logical_or(jnp.logical_and(middle, lane >= CZ), jnp.logical_and(jnp.logical_not(middle), lane < LANES - CZ))
    open_z = jnp.logical_or(jnp.logical_and(bottom, layer > 0), jnp.logical_and(jnp.logical_not(bottom), layer < CZ - 1))

    def coarse_coefficients(block, carry):
        wide = flows[block]
        center = jnp.ones((ROWS, 8, LANES), jnp.float32)
        for axis in range(3):
            slope = signs[axis] * wide[:, axis]
            jump = jnp.minimum(-slope, 0.0)
            center = center + H * (0.5 * slope + jump)
            coef[1 + axis, block] = (-0.5 * H) * slope
            outer = -H * jump
            if axis == 1:
                outer = jnp.where(open_y, outer, 0.0)
            if axis == 2:
                outer = jnp.where(open_z, outer, 0.0)
            coef[4 + axis, block] = outer
        coef[0, block] = center
        return carry

    lax.fori_loop(0, 2 * REACH + 1, coarse_coefficients, 0)

    def advance(u, low):
        count = u.shape[0]
        own = u[1 : count - 1]
        px = pltpu.roll(u, 4, 1)
        ox = jnp.where(top, px[0 : count - 2], px[2:count])
        px = px[1 : count - 1]
        py = jnp.where(middle, pltpu.roll(own, 6, 1), pltpu.roll(own, 2, 1))
        pz = jnp.where(bottom, pltpu.roll(own, 7, 1), pltpu.roll(own, 1, 1))
        oy = jnp.where(middle, pltpu.roll(py, CZ, 2), pltpu.roll(py, LANES - CZ, 2))
        oz = jnp.where(bottom, pltpu.roll(pz, 1, 2), pltpu.roll(pz, LANES - 1, 2))
        total = None
        for index, value in enumerate((own, px, py, pz, ox, oy, oz)):
            factors = coef[index].reshape(SPAN, 8, LANES)[low + 1 : low + count - 1]
            piece = factors * value
            total = piece if total is None else total + piece
        return total

    res_same = [split(RES[0, 2 * i], RES[1, 2 * i + 1]) for i in range(2)]
    res_cross = [split(RES[0, 2 * i + 1], RES[1, 2 * i]) for i in range(2)]
    pro_same = [split(PRO[2 * i, 0], PRO[2 * i + 1, 1]) for i in range(2)]
    pro_cross = [split(PRO[2 * i, 1], PRO[2 * i + 1, 0]) for i in range(2)]

    def restricted(field):
        for i in range(2):
            lines = weighted([(RES[i, a], field[a]) for a in range(4)])
            for j in range(2):
                pair = weighted([(RES[j, b], lines[b]) for b in range(4)])
                turned = pltpu.roll(pair, 4, 1)
                value = (
                    res_same[0] * pair[0]
                    + res_cross[0] * turned[0]
                    + res_same[1] * pair[1]
                    + res_cross[1] * turned[1]
                )
                shuffle[pl.ds(8 * (2 * i + j), 8)] = value
        return jnp.stack([shuffle[pl.ds(r, 8, stride=4)] for r in range(ROWS)])

    def prolonged(rows):
        for r in range(ROWS):
            shuffle[pl.ds(r, 8, stride=4)] = rows[r]
        corners = []
        for index in range(4):
            value = shuffle[pl.ds(8 * index, 8)]
            turned = pltpu.roll(value, 4, 0)
            corners.append(jnp.stack([pro_same[i] * value + pro_cross[i] * turned for i in range(2)]))
        lines = [
            jnp.stack([weighted([(PRO[b, 0], corners[2 * i]), (PRO[b, 1], corners[2 * i + 1])]) for b in range(4)])
            for i in range(2)
        ]
        return [weighted([(PRO[a, 0], lines[0]), (PRO[a, 1], lines[1])]) for a in range(4)]

    arrive("begin_trace")
    for _, receives, make, _ in transfers["first_trace"]:
        when(receives, lambda make=make: make().wait_recv())
    arrive("begin")
    interior(begin, first_rate)
    lower, upper = finish_rate(first_rate, 3)

    def fine_copy(k, d, slot):
        return remote(
            send.at[k, slot],
            recv.at[1 - k, slot],
            fine_send.at[k, slot],
            fine_recv.at[1 - k, slot],
            (n, s + d),
        )

    def launch(slot):
        for k, d in enumerate((-1, 1)):
            pl.when(has[d])(lambda k=k, d=d: fine_copy(k, d, slot).start())

    def await_fine(slot):
        for k, d in enumerate((-1, 1)):
            pl.when(has[-d])(lambda k=k, d=d: fine_copy(k, d, slot).wait_recv())

    def fresh(u, origin, factor, rate, lower, upper, slot):
        first = origin[0] + factor * lower
        last = origin[3] + factor * upper
        u[0] = first
        u[3] = last
        pack(first, last, slot)
        launch(slot)
        u[1:3] = origin[1:3] + factor * rate[1:3]

    base[...] = base[...] + begin[...]
    fresh(mid_state, base, DT, first_rate, lower, upper, 4)

    def to_closing(slot):
        base[...] = (
            mid_state[...]
            - DT * rates[1]
            + (H / 24.0) * (8.0 * rates[1] + 5.0 * rates[2] - rates[0])
        )
        interior(mid_state, rates.at[1])
        await_fine(slot)
        lower, upper = finish_rate(rates.at[1], slot)
        fresh(end_state, base, DT, rates.at[1], lower, upper, slot + 1)

    to_closing(4)
    rates[0] = first_rate[...]

    old0[1 : ROWS + 1] = restricted(begin)
    start("row0")

    def sweep(index, carry):
        slot = 5 + 2 * index
        base[...] = begin[...] + (H / 24.0) * (5.0 * first_rate[...] + 8.0 * rates[1])
        interior(end_state, rates.at[2])
        await_fine(slot)
        lower, upper = finish_rate(rates.at[2], slot)
        fresh(mid_state, base, -H / 24.0, rates.at[2], lower, upper, slot + 1)
        to_closing(slot + 1)
        return carry

    lax.fori_loop(0, 2, sweep, 0)

    old1[1 : ROWS + 1] = restricted(end_state)
    start("row1")
    arrive("row0")
    low = MID - 1
    before0 = old0[1 : ROWS + 1]
    h_rate0 = advance(old0[...], low) - before0
    interior(end_state, rates.at[2])
    await_fine(9)
    finish_rate(rates.at[2], 9)
    quadrature = restricted(
        [(H / 6.0) * (first_rate[a] + 4.0 * rates[1, a] + rates[2, a]) for a in range(4)]
    )
    arrive("row1")
    before1 = old1[1 : ROWS + 1]
    h_rate1 = advance(old1[...], low) - before1
    trapezoid = 0.5 * (h_rate0 + h_rate1)
    offset = -h_rate0 + trapezoid + (quadrature - trapezoid)
    is_first = n == 0
    offset = offset + jnp.where(is_first, before0 + h_rate0, 0.0)

    group[z, pl.ds(ROWS, ROWS)] = offset
    start("group")
    arrive("group")
    start("side")
    arrive("side")
    y = group[0]
    y = advance(y, MID - 4) + group[1, 1:11]
    y = advance(y, MID - 3) + group[2, 2:10]
    y = advance(y, MID - 2)[1:5] + group[3, 4:8]
    partial[...] = y
    start("part")
    arrive("part")
    y = far[...]
    for step in range(4):
        y = advance(y, step)
    y = y + mid[...]
    for step in range(4, 8):
        y = advance(y, step)
    y = y + near[...]
    for j in range(3):
        count = 12 - 2 * j
        stepped = advance(y, MID - 4 + j) + group[j, j + 1 : 11 - j]
        y = jnp.where(z > j, stepped, y[1 : count - 1])
    finish = advance(y, MID - 1) + group[z, pl.ds(ROWS, ROWS)]
    begin_rows = jnp.where(is_first, before0, y[1:5])
    delta0 = begin_rows - before0
    delta1 = finish - before1

    for index, (delta, field) in enumerate(
        ((delta0, begin), (0.5 * (delta0 + delta1), mid_state), (delta1, end_state))
    ):
        lifted = prolonged(delta)
        for a in range(4):
            result[index, a] = field[a] + lifted[a]
        pltpu.make_async_copy(result.at[index], out_hbm.at[index], store_sem.at[index]).start()
    for index in range(3):
        pltpu.make_async_copy(result.at[index], out_hbm.at[index], store_sem.at[index]).wait()

    for name in transfers:
        sent(name)
    for k, d in enumerate((-1, 1)):
        for slot in range(4, 10):
            pl.when(has[d])(lambda k=k, d=d, slot=slot: fine_copy(k, d, slot).wait_send())


def solution(mesh):
    steps = mesh.shape["tm"]
    columns = mesh.shape["space"]

    def body(node_states, initial_state, velocity):
        states = node_states.reshape((3,) + FIELD)
        first = initial_state.reshape(FIELD)
        wind = velocity.reshape(3, 4, 4, 16, LANES)
        f32 = jnp.float32
        vmem = lambda *shape: pltpu.VMEM(shape, f32)
        dma = lambda *shape: pltpu.SemaphoreType.DMA(shape)
        out = pl.pallas_call(
            functools.partial(kernel, steps, columns),
            out_shape=jax.ShapeDtypeStruct((3,) + FIELD, f32),
            in_specs=[pl.BlockSpec(memory_space=pl.ANY)] * 3,
            out_specs=pl.BlockSpec(memory_space=pl.ANY),
            scratch_shapes=[
                vmem(3, *FIELD),
                pltpu.VMEM((3, 4, 4, 16, LANES), jnp.bfloat16),
                vmem(*FIELD),
                vmem(3, *FIELD),
                vmem(*FIELD),
                vmem(4, 2, 8, LANES),
                vmem(4, 2, 8, LANES),
                vmem(4, 2, 8, LANES),
                vmem(4, 2, 8, LANES),
                vmem(4, 2, 8, LANES),
                vmem(4, 2, 8, LANES),
                vmem(4, 4, 8, LANES),
                vmem(4, 4, 8, LANES),
                vmem(3, *FIELD),
                vmem(*FIELD),
                vmem(*FIELD),
                vmem(*FIELD),
                vmem(*FIELD),
                vmem(2, 10, 2, 8, LANES),
                vmem(2, 10, 2, 8, LANES),
                vmem(32, LANES),
                vmem(2 * REACH + 1, ROWS, 3, 8, LANES),
                vmem(7, 2 * REACH + 1, ROWS, 8, LANES),
                vmem(ROWS + 2, 8, LANES),
                vmem(ROWS + 2, 8, LANES),
                vmem(GROUP, 3 * ROWS, 8, LANES),
                vmem(ROWS, 8, LANES),
                vmem(3 * ROWS, 8, LANES),
                vmem(5 * ROWS, 8, LANES),
                vmem(7 * ROWS, 8, LANES),
                vmem(3, *FIELD),
                dma(3),
                dma(3),
                dma(2, 10),
                dma(2, 10),
                pltpu.SemaphoreType.DMA,
                pltpu.SemaphoreType.DMA,
                dma(6),
                dma(6),
                dma(2, 2),
                dma(2, 2),
                dma(3),
                dma(3),
                dma(2),
                dma(2),
                dma(15),
                dma(15),
            ],
            compiler_params=pltpu.CompilerParams(
                collective_id=0, has_side_effects=True, vmem_limit_bytes=32 * 1024 * 1024
            ),
        )(states, first, wind)
        return out.reshape(1, 3, 64, ROWS, LANES)

    return jax.shard_map(
        body,
        mesh=mesh,
        in_specs=(
            P("tm", None, None, "space", None),
            P(None, "space", None),
            P(None, None, "space", None),
        ),
        out_specs=P("tm", None, None, "space", None),
        check_vma=False,
    )
```

time: 433 us -> 73.8 us (0.17)
  the two profiles are of different devices: /device:TPU:95 before, /device:TPU:57 now
where the time goes in v1:
time: 73.8 us; the launch traced here: 73.6 us
  Pallas kernels  70 us (95%)
  local copies, waits for them, and re-layouts  3.57 us (5%)
    pallas_call x1, Pallas kernels, body(): pl.pallas_call(functools.partial(kernel, steps, columns), out_shape=jax.S...  70 us
    unnamed x7, local copies, waits for them, and re-layouts  3.57 us

profile of v1, /device:TPU:57, one launch (start us, length us, event | category | flops | bytes accessed | tf_op | source)
XLA Modules:
  0.0 73.6 jit_solution(16346381736012069324)
XLA Ops:
  0.0 0.0 copy-start
  0.0 1.0 %copy-done = f32[1,3,64,4,128]{4,3,2,1,0:T(4,128)S(1)} copy-done((f32[1,3,64,4,128]{4,3,2,1,0:T(4,128)S(1)}, f32[1,3,64,4,128]{4,3,2,1,0:T(4,128)}, u32[]{:S(2)}) %copy-start) | copy-done | bytes 393240
  1.0 0.0 copy-start.1
  1.0 0.9 %copy-done.1 = bf16[3,64,4,128]{3,2,1,0:T(4,128)(2,1)S(1)} copy-done((bf16[3,64,4,128]{3,2,1,0:T(4,128)(2,1)S(1)}, bf16[3,64,4,128]{3,2,1,0:T(4,128)(2,1)}, u32[]{:S(2)}) %copy-start.1) | copy-done | bytes 196632
  1.9 0.0 copy-start.2
  1.9 0.9 %copy-done.2 = f32[64,4,128]{2,1,0:T(4,128)S(1)} copy-done((f32[64,4,128]{2,1,0:T(4,128)S(1)}, f32[64,4,128]{2,1,0:T(4,128)}, u32[]{:S(2)}) %copy-start.2) | copy-done | bytes 131096
  2.8 70.0 %shard_map.37 = f32[3,4,4,2,8,128]{5,4,3,2,1,0:T(8,128)S(1)} custom-call(f32[3,4,4,2,8,128]{5,4,3,2,1,0:T(8,128)S(1)} %bitcast.5, f32[4,4,2,8,128]{4,3,2,1,0:T(8,128)S(1)} %bitcast.7, bf16[3,4,4,16,128]{4,3,2,1,0:T(8,128)(2,1)S(1)} %bitcast.6), custom_call_target="tpu_custom_call" | custom-call | tf_op jit(solution)/shard_map/pallas_call | solution.py:690
  72.8 0.7 %copy.5 = f32[1,3,64,4,128]{4,3,2,1,0:T(4,128)} copy(f32[1,3,64,4,128]{4,3,2,1,0:T(4,128)S(1)} %bitcast.4) | data formatting | bytes 786432
Async XLA Ops:
  0.0 1.0 %copy-start = (f32[1,3,64,4,128]{4,3,2,1,0:T(4,128)S(1)}, f32[1,3,64,4,128]{4,3,2,1,0:T(4,128)}, u32[]{:S(2)}) copy-start(f32[1,3,64,4,128]{4,3,2,1,0:T(4,128)} %param.3) | copy-start | bytes 1179652
  1.0 0.9 %copy-start.1 = (bf16[3,64,4,128]{3,2,1,0:T(4,128)(2,1)S(1)}, bf16[3,64,4,128]{3,2,1,0:T(4,128)(2,1)}, u32[]{:S(2)}) copy-start(bf16[3,64,4,128]{3,2,1,0:T(4,128)(2,1)} %param.5) | copy-start | bytes 589828
  1.9 0.9 %copy-start.2 = (f32[64,4,128]{2,1,0:T(4,128)S(1)}, f32[64,4,128]{2,1,0:T(4,128)}, u32[]{:S(2)}) copy-start(f32[64,4,128]{2,1,0:T(4,128)} %param.4) | copy-start | bytes 393220

commit v2 on v1

--- a/solution.py
+++ b/solution.py
@@ -366,11 +366,12 @@
         load_first.wait()
         pack(begin[0], begin[3], 3)
 
-    pl.semaphore_wait(barrier, expected)
-    start("begin_trace")
-    start("first_trace")
-    start("begin")
-    start("states")
+    with jax.named_scope("greet"):
+        pl.semaphore_wait(barrier, expected)
+        start("begin_trace")
+        start("first_trace")
+        start("begin")
+        start("states")
 
     load_wind.wait()
     for axis in range(3):
@@ -461,12 +462,13 @@
         interior(states.at[k], rates.at[k])
         return carry
 
-    lax.fori_loop(0, 3, old_rate, 0)
-    arrive("states")
-    for k in range(3):
-        finish_rate(rates.at[k], k)
-
-    base[...] = -DT * rates[0] + (H / 24.0) * (5.0 * rates[0] + 8.0 * rates[1] - rates[2])
+    with jax.named_scope("old_rates"):
+        lax.fori_loop(0, 3, old_rate, 0)
+        arrive("states")
+        for k in range(3):
+            finish_rate(rates.at[k], k)
+
+        base[...] = -DT * rates[0] + (H / 24.0) * (5.0 * rates[0] + 8.0 * rates[1] - rates[2])
 
     arrive("flow")
     top = (sub // 4) % 2 == 0
@@ -546,12 +548,13 @@
         ]
         return [weighted([(PRO[a, 0], lines[0]), (PRO[a, 1], lines[1])]) for a in range(4)]
 
-    arrive("begin_trace")
-    for _, receives, make, _ in transfers["first_trace"]:
-        when(receives, lambda make=make: make().wait_recv())
-    arrive("begin")
-    interior(begin, first_rate)
-    lower, upper = finish_rate(first_rate, 3)
+    with jax.named_scope("begin_arrives"):
+        arrive("begin_trace")
+        for _, receives, make, _ in transfers["first_trace"]:
+            when(receives, lambda make=make: make().wait_recv())
+        arrive("begin")
+        interior(begin, first_rate)
+        lower, upper = finish_rate(first_rate, 3)
 
     def fine_copy(k, d, slot):
         return remote(
@@ -579,8 +582,9 @@
         launch(slot)
         u[1:3] = origin[1:3] + factor * rate[1:3]
 
-    base[...] = base[...] + begin[...]
-    fresh(mid_state, base, DT, first_rate, lower, upper, 4)
+    with jax.named_scope("first_middle"):
+        base[...] = base[...] + begin[...]
+        fresh(mid_state, base, DT, first_rate, lower, upper, 4)
 
     def to_closing(slot):
         base[...] = (
@@ -593,8 +597,9 @@
         lower, upper = finish_rate(rates.at[1], slot)
         fresh(end_state, base, DT, rates.at[1], lower, upper, slot + 1)
 
-    to_closing(4)
-    rates[0] = first_rate[...]
+    with jax.named_scope("first_closing"):
+        to_closing(4)
+        rates[0] = first_rate[...]
 
     old0[1 : ROWS + 1] = restricted(begin)
     start("row0")
@@ -609,65 +614,77 @@
         to_closing(slot + 1)
         return carry
 
-    lax.fori_loop(0, 2, sweep, 0)
-
-    old1[1 : ROWS + 1] = restricted(end_state)
-    start("row1")
-    arrive("row0")
-    low = MID - 1
-    before0 = old0[1 : ROWS + 1]
-    h_rate0 = advance(old0[...], low) - before0
-    interior(end_state, rates.at[2])
-    await_fine(9)
-    finish_rate(rates.at[2], 9)
-    quadrature = restricted(
-        [(H / 6.0) * (first_rate[a] + 4.0 * rates[1, a] + rates[2, a]) for a in range(4)]
-    )
-    arrive("row1")
-    before1 = old1[1 : ROWS + 1]
-    h_rate1 = advance(old1[...], low) - before1
-    trapezoid = 0.5 * (h_rate0 + h_rate1)
-    offset = -h_rate0 + trapezoid + (quadrature - trapezoid)
-    is_first = n == 0
-    offset = offset + jnp.where(is_first, before0 + h_rate0, 0.0)
-
-    group[z, pl.ds(ROWS, ROWS)] = offset
-    start("group")
-    arrive("group")
-    start("side")
-    arrive("side")
-    y = group[0]
-    y = advance(y, MID - 4) + group[1, 1:11]
-    y = advance(y, MID - 3) + group[2, 2:10]
-    y = advance(y, MID - 2)[1:5] + group[3, 4:8]
-    partial[...] = y
-    start("part")
-    arrive("part")
-    y = far[...]
-    for step in range(4):
-        y = advance(y, step)
-    y = y + mid[...]
-    for step in range(4, 8):
-        y = advance(y, step)
-    y = y + near[...]
-    for j in range(3):
-        count = 12 - 2 * j
-        stepped = advance(y, MID - 4 + j) + group[j, j + 1 : 11 - j]
-        y = jnp.where(z > j, stepped, y[1 : count - 1])
-    finish = advance(y, MID - 1) + group[z, pl.ds(ROWS, ROWS)]
-    begin_rows = jnp.where(is_first, before0, y[1:5])
-    delta0 = begin_rows - before0
-    delta1 = finish - before1
-
-    for index, (delta, field) in enumerate(
-        ((delta0, begin), (0.5 * (delta0 + delta1), mid_state), (delta1, end_state))
-    ):
-        lifted = prolonged(delta)
-        for a in range(4):
-            result[index, a] = field[a] + lifted[a]
-        pltpu.make_async_copy(result.at[index], out_hbm.at[index], store_sem.at[index]).start()
-    for index in range(3):
-        pltpu.make_async_copy(result.at[index], out_hbm.at[index], store_sem.at[index]).wait()
+    with jax.named_scope("sweeps"):
+        lax.fori_loop(0, 2, sweep, 0)
+
+    with jax.named_scope("offset"):
+        old1[1 : ROWS + 1] = restricted(end_state)
+        start("row1")
+        arrive("row0")
+        low = MID - 1
+        before0 = old0[1 : ROWS + 1]
+        h_rate0 = advance(old0[...], low) - before0
+        interior(end_state, rates.at[2])
+        await_fine(9)
+        finish_rate(rates.at[2], 9)
+        quadrature = restricted(
+            [(H / 6.0) * (first_rate[a] + 4.0 * rates[1, a] + rates[2, a]) for a in range(4)]
+        )
+        arrive("row1")
+        before1 = old1[1 : ROWS + 1]
+        h_rate1 = advance(old1[...], low) - before1
+        trapezoid = 0.5 * (h_rate0 + h_rate1)
+        offset = -h_rate0 + trapezoid + (quadrature - trapezoid)
+        is_first = n == 0
+        offset = offset + jnp.where(is_first, before0 + h_rate0, 0.0)
+
+    with jax.named_scope("gather_offsets"):
+        group[z, pl.ds(ROWS, ROWS)] = offset
+        start("group")
+        arrive("group")
+
+    with jax.named_scope("side_rows"):
+        start("side")
+        arrive("side")
+
+    with jax.named_scope("group_sum"):
+        y = group[0]
+        y = advance(y, MID - 4) + group[1, 1:11]
+        y = advance(y, MID - 3) + group[2, 2:10]
+        y = advance(y, MID - 2)[1:5] + group[3, 4:8]
+        partial[...] = y
+        start("part")
+
+    with jax.named_scope("sums_arrive"):
+        arrive("part")
+
+    with jax.named_scope("coarse_chain"):
+        y = far[...]
+        for step in range(4):
+            y = advance(y, step)
+        y = y + mid[...]
+        for step in range(4, 8):
+            y = advance(y, step)
+        y = y + near[...]
+        for j in range(3):
+            count = 12 - 2 * j
+            stepped = advance(y, MID - 4 + j) + group[j, j + 1 : 11 - j]
+            y = jnp.where(z > j, stepped, y[1 : count - 1])
+        finish = advance(y, MID - 1) + group[z, pl.ds(ROWS, ROWS)]
+        begin_rows = jnp.where(is_first, before0, y[1:5])
+        delta0 = begin_rows - before0
+        delta1 = finish - before1
+
+    with jax.named_scope("output"):
+        for index, (delta, field) in enumerate(
+            ((delta0, begin), (0.5 * (delta0 + delta1), mid_state), (delta1, end_state))
+        ):
+            lifted = prolonged(delta)
+            for a in range(4):
+                result[index, a] = field[a] + lifted[a]
+            pltpu.make_async_copy(result.at[index], out_hbm.at[index], store_sem.at[index]).start()
+        for index in range(3):
+            pltpu.make_async_copy(result.at[index], out_hbm.at[index], store_sem.at[index]).wait()
 
     for name in transfers:
         sent(name)
@@ -690,7 +707,7 @@
         out = pl.pallas_call(
             functools.partial(kernel, steps, columns),
             out_shape=jax.ShapeDtypeStruct((3,) + FIELD, f32),
-            in_specs=[pl.BlockSpec(memory_space=pl.ANY)] * 3,
+            in_specs=[pl.BlockSpec(memory_space=pltpu.HBM)] * 3,
             out_specs=pl.BlockSpec(memory_space=pl.ANY),
             scratch_shapes=[
                 vmem(3, *FIELD),
@@ -742,7 +759,7 @@
                 dma(15),
             ],
             compiler_params=pltpu.CompilerParams(
-                collective_id=0, has_side_effects=True, vmem_limit_bytes=32 * 1024 * 1024
+                collective_id=0, has_side_effects=True, vmem_limit_bytes=60 * 1024 * 1024
             ),
         )(states, first, wind)
         return out.reshape(1, 3, 64, ROWS, LANES)

time: 73.8 us -> 71.6 us (0.970)
  local copies, waits for them, and re-layouts: 3.57 us -> 1.77 us
    unnamed x7 -> x1, local copies, waits for them, and re-layouts: 3.57 us -> 1.77 us
where the time goes in v2:
time: 71.6 us; the launch traced here: 71.5 us
  Pallas kernels  69.7 us (97%)
  local copies, waits for them, and re-layouts  1.77 us (2%)
    pallas_call x1, Pallas kernels, body(): pl.pallas_call(functools.partial(kernel, steps, columns), out_shape=jax.S...  69.7 us
    unnamed x1, local copies, waits for them, and re-layouts  1.77 us

profile of v2, /device:TPU:57, one launch (start us, length us, event | category | flops | bytes accessed | tf_op | source)
XLA Modules:
  0.0 71.5 jit_solution(2321513054024812955)
XLA Ops:
  0.0 69.7 %shard_map.37 = f32[3,4,4,2,8,128]{5,4,3,2,1,0:T(8,128)} custom-call(f32[3,4,4,2,8,128]{5,4,3,2,1,0:T(8,128)} %bitcast.5, f32[4,4,2,8,128]{4,3,2,1,0:T(8,128)} %bitcast.7, bf16[3,4,4,16,128]{4,3,2,1,0:T(8,128)(2,1)} %bitcast.6), custom_call_target="tpu_custom_call" | custom-call | tf_op jit(solution)/shard_map/pallas_call | solution.py:707
  69.7 1.8 %copy.5 = f32[1,3,64,4,128]{4,3,2,1,0:T(4,128)} copy(f32[1,3,64,4,128]{4,3,2,1,0:T(4,128)} %bitcast.4) | data formatting | bytes 786432

commit v3 on v1

--- a/solution.py
+++ b/solution.py
@@ -233,10 +233,11 @@
         (n - 1, s),
     )
     for index, d in enumerate((-3, -2, -1, 1, 2, 3)):
+        needed = None if abs(d) == 1 else g >= abs(d)
         add(
-            "flow",
-            inside(d),
-            inside(-d),
+            f"flow{abs(d)}",
+            both(needed, inside(d)),
+            both(needed, inside(-d)),
             functools.partial(
                 remote,
                 flows.at[REACH],
@@ -263,7 +264,7 @@
             (g * GROUP + (z + GROUP - shift) % GROUP, s),
         )
     slot = 0
-    for distance, buffer in ((1, near), (2, mid), (3, far)):
+    for distance, buffer in ((3, far), (2, mid), (1, near)):
         for d in range(-distance, distance + 1):
             add(
                 "part",
@@ -321,10 +322,8 @@
     for d in (-1, 1):
         greet(has[d], (n, s + d))
         expected = expected + has[d].astype(jnp.int32)
-    for name in ("begin_trace", "begin", "flow", "group", "part"):
-        for index, (sends, receives, _, partner) in enumerate(transfers[name]):
-            if name == "flow" and index in (2, 3):
-                continue
+    for name in ("begin_trace", "begin", "flow2", "flow3", "group", "part"):
+        for sends, receives, _, partner in transfers[name]:
             greet(receives, partner)
             expected = expected + (1 if sends is None else sends.astype(jnp.int32))
 
@@ -383,7 +382,6 @@
                 shuffle[pl.ds(8 * (2 * i + j), 8)] = corner
         for r in range(ROWS):
             flows[REACH, r, axis] = shuffle[pl.ds(r, 8, stride=4)]
-    start("flow")
 
     cxl = LIFT * jnp.minimum(nv[0, 0], 0.0)
     cxh = LIFT * jnp.minimum(-nv[0, 3], 0.0)
@@ -468,7 +466,6 @@
 
     base[...] = -DT * rates[0] + (H / 24.0) * (5.0 * rates[0] + 8.0 * rates[1] - rates[2])
 
-    arrive("flow")
     top = (sub // 4) % 2 == 0
     middle = (sub // 2) % 2 == 0
     bottom = sub % 2 == 0
@@ -493,8 +490,6 @@
         coef[0, block] = center
         return carry
 
-    lax.fori_loop(0, 2 * REACH + 1, coarse_coefficients, 0)
-
     def advance(u, low):
         count = u.shape[0]
         own = u[1 : count - 1]
@@ -593,11 +588,13 @@
         lower, upper = finish_rate(rates.at[1], slot)
         fresh(end_state, base, DT, rates.at[1], lower, upper, slot + 1)
 
+    start("flow1")
     to_closing(4)
     rates[0] = first_rate[...]
 
     old0[1 : ROWS + 1] = restricted(begin)
     start("row0")
+    start("flow2")
 
     def sweep(index, carry):
         slot = 5 + 2 * index
@@ -609,15 +606,19 @@
         to_closing(slot + 1)
         return carry
 
-    lax.fori_loop(0, 2, sweep, 0)
+    sweep(0, 0)
+    start("flow3")
+    sweep(1, 0)
 
     old1[1 : ROWS + 1] = restricted(end_state)
     start("row1")
-    arrive("row0")
+    interior(end_state, rates.at[2])
+    for name in ("flow1", "flow2", "flow3", "row0"):
+        arrive(name)
+    lax.fori_loop(0, 2 * REACH + 1, coarse_coefficients, 0)
     low = MID - 1
     before0 = old0[1 : ROWS + 1]
     h_rate0 = advance(old0[...], low) - before0
-    interior(end_state, rates.at[2])
     await_fine(9)
     finish_rate(rates.at[2], 9)
     quadrature = restricted(
@@ -690,7 +691,7 @@
         out = pl.pallas_call(
             functools.partial(kernel, steps, columns),
             out_shape=jax.ShapeDtypeStruct((3,) + FIELD, f32),
-            in_specs=[pl.BlockSpec(memory_space=pl.ANY)] * 3,
+            in_specs=[pl.BlockSpec(memory_space=pltpu.HBM)] * 3,
             out_specs=pl.BlockSpec(memory_space=pl.ANY),
             scratch_shapes=[
                 vmem(3, *FIELD),
@@ -742,7 +743,7 @@
                 dma(15),
             ],
             compiler_params=pltpu.CompilerParams(
-                collective_id=0, has_side_effects=True, vmem_limit_bytes=32 * 1024 * 1024
+                collective_id=0, has_side_effects=True, vmem_limit_bytes=60 * 1024 * 1024
             ),
         )(states, first, wind)
         return out.reshape(1, 3, 64, ROWS, LANES)

time: 73.8 us -> 68.8 us (0.932)
  the two profiles are of different devices: /device:TPU:57 before, /device:TPU:104 now
where the time goes in v3:
time: 68.8 us; the launch traced here: 68.6 us
  Pallas kernels  66.8 us (97%)
  local copies, waits for them, and re-layouts  1.77 us (3%)
    pallas_call x1, Pallas kernels, body(): pl.pallas_call(functools.partial(kernel, steps, columns), out_shape=jax.S...  66.8 us
    unnamed x1, local copies, waits for them, and re-layouts  1.77 us

profile of v3, /device:TPU:104, one launch (start us, length us, event | category | flops | bytes accessed | tf_op | source)
XLA Modules:
  0.0 68.6 jit_solution(15105881767219761783)
XLA Ops:
  0.0 66.8 %shard_map.37 = f32[3,4,4,2,8,128]{5,4,3,2,1,0:T(8,128)} custom-call(f32[3,4,4,2,8,128]{5,4,3,2,1,0:T(8,128)} %bitcast.5, f32[4,4,2,8,128]{4,3,2,1,0:T(8,128)} %bitcast.7, bf16[3,4,4,16,128]{4,3,2,1,0:T(8,128)(2,1)} %bitcast.6), custom_call_target="tpu_custom_call" | custom-call | tf_op jit(solution)/shard_map/pallas_call | solution.py:691
  66.8 1.8 %copy.5 = f32[1,3,64,4,128]{4,3,2,1,0:T(4,128)} copy(f32[1,3,64,4,128]{4,3,2,1,0:T(4,128)} %bitcast.4) | data formatting | bytes 786432

commit v4 on v3

--- a/solution.py
+++ b/solution.py
@@ -81,6 +81,16 @@
     base,
     send,
     recv,
+    duo_begin,
+    duo_first,
+    duo_rates,
+    duo_mid,
+    duo_end,
+    duo_base,
+    duo_send,
+    duo_recv,
+    leaving,
+    passed,
     shuffle,
     flows,
     coef,
@@ -96,6 +106,10 @@
     store_sem,
     fine_send,
     fine_recv,
+    duo_out,
+    duo_in,
+    hop_send,
+    hop_recv,
     begin_send,
     begin_recv,
     flow_send,
@@ -203,34 +217,52 @@
                 has[-d],
                 functools.partial(
                     remote,
-                    buffer.at[1 if d < 0 else ROWS],
-                    buffer.at[ROWS + 1 if d < 0 else 0],
+                    buffer.at[:, 1 if d < 0 else ROWS],
+                    buffer.at[:, ROWS + 1 if d < 0 else 0],
                     row_send.at[k, index],
                     row_recv.at[1 - k, index],
                     (n, s + d),
                 ),
                 None,
             )
+        for shift in range(GROUP):
+            part_of = (z + GROUP - shift) % GROUP
+            add(
+                f"side{shift}",
+                has[d],
+                has[-d],
+                functools.partial(
+                    remote,
+                    group.at[part_of, pl.ds(ROWS, ROWS)],
+                    group.at[part_of, pl.ds(2 * ROWS if d < 0 else 0, ROWS)],
+                    side_send.at[k, shift],
+                    side_recv.at[1 - k, shift],
+                    (n, s + d),
+                ),
+                None,
+            )
+    for piece in range(8):
+        where_to = (piece // 2, pl.ds(2 * (piece % 2), 2))
         add(
-            "side",
-            has[d],
-            has[-d],
+            f"begin{piece}",
+            n < steps - 1,
+            n > 0,
             functools.partial(
                 remote,
-                group.at[:, pl.ds(ROWS, ROWS)],
-                group.at[:, pl.ds(2 * ROWS if d < 0 else 0, ROWS)],
-                side_send.at[k],
-                side_recv.at[1 - k],
-                (n, s + d),
+                states_hbm.at[(2,) + where_to],
+                begin.at[where_to],
+                begin_send.at[piece],
+                begin_recv.at[piece],
+                (n + 1, s),
             ),
-            None,
+            (n - 1, s),
         )
     add(
-        "begin",
+        "hop",
         n < steps - 1,
         n > 0,
-        functools.partial(remote, states_hbm.at[2], begin, begin_send, begin_recv, (n + 1, s)),
-        (n - 1, s),
+        functools.partial(remote, leaving, passed, hop_send, hop_recv, (n + 1, s)),
+        None,
     )
     for index, d in enumerate((-3, -2, -1, 1, 2, 3)):
         needed = None if abs(d) == 1 else g >= abs(d)
@@ -302,6 +334,10 @@
     pl.when(n == 0)(load_first.start)
 
     recv[...] = jnp.zeros(recv.shape, jnp.float32)
+    duo_recv[...] = jnp.zeros(duo_recv.shape, jnp.float32)
+    passed[...] = jnp.zeros(passed.shape, jnp.float32)
+    duo_begin[0] = jnp.zeros(FIELD, jnp.float32)
+    duo_first[0] = jnp.zeros(FIELD, jnp.float32)
     flows[...] = jnp.zeros(flows.shape, jnp.float32)
     old0[...] = jnp.zeros(old0.shape, jnp.float32)
     old1[...] = jnp.zeros(old1.shape, jnp.float32)
@@ -322,14 +358,14 @@
     for d in (-1, 1):
         greet(has[d], (n, s + d))
         expected = expected + has[d].astype(jnp.int32)
-    for name in ("begin_trace", "begin", "flow2", "flow3", "group", "part"):
+    for name in ("begin_trace", "begin0", "flow2", "flow3", "group", "part"):
         for sends, receives, _, partner in transfers[name]:
             greet(receives, partner)
             expected = expected + (1 if sends is None else sends.astype(jnp.int32))
 
     load_states.wait()
 
-    def pack(lower, upper, k_slot):
+    def pack(lower, upper, low_to, high_to):
         for half in range(2):
             low = None
             high = None
@@ -341,15 +377,15 @@
                 hv = pltpu.roll(hv, (r + 5) % 8, 0) if r != 3 else hv
                 low = lv if low is None else jnp.where(row == r, lv, low)
                 high = hv if high is None else jnp.where(row == r, hv, high)
-            send[0, k_slot, half] = low
-            send[1, k_slot, half] = high
-
-    def unpack(k_slot):
+            low_to[half] = low
+            high_to[half] = high
+
+    def unpack(low_from, high_from):
         lows, highs = [], []
         for t in range(8):
             half, r = t // 4, t % 4
-            lv = recv[0, k_slot, half]
-            hv = recv[1, k_slot, half]
+            lv = low_from[half]
+            hv = high_from[half]
             lows.append(pltpu.roll(lv, 8 - r, 0) if r else lv)
             highs.append(pltpu.roll(hv, 3 - r, 0) if r != 3 else hv)
         return (
@@ -358,18 +394,19 @@
         )
 
     for k in range(3):
-        pack(states[k, 0], states[k, 3], k)
+        pack(states[k, 0], states[k, 3], send.at[0, k], send.at[1, k])
 
     @pl.when(n == 0)
     def _():
         load_first.wait()
-        pack(begin[0], begin[3], 3)
+        pack(begin[0], begin[3], send.at[0, 3], send.at[1, 3])
 
     pl.semaphore_wait(barrier, expected)
     start("begin_trace")
     start("first_trace")
-    start("begin")
     start("states")
+    start("begin0")
+    start("begin1")
 
     load_wind.wait()
     for axis in range(3):
@@ -447,8 +484,8 @@
             out[2, b] = total[2]
             out[3, b] = total[3] + xhi[b] * pltpu.roll(ub[0], 7, 1)
 
-    def finish_rate(out, k_slot):
-        low, high = unpack(k_slot)
+    def finish_rate(out, low_from, high_from):
+        low, high = unpack(low_from, high_from)
         lower = out[0] + xlh[...] * low
         upper = out[3] + xhh[...] * high
         out[0] = lower
@@ -462,7 +499,7 @@
     lax.fori_loop(0, 3, old_rate, 0)
     arrive("states")
     for k in range(3):
-        finish_rate(rates.at[k], k)
+        finish_rate(rates.at[k], recv.at[0, k], recv.at[1, k])
 
     base[...] = -DT * rates[0] + (H / 24.0) * (5.0 * rates[0] + 8.0 * rates[1] - rates[2])
 
@@ -541,12 +578,153 @@
         ]
         return [weighted([(PRO[a, 0], lines[0]), (PRO[a, 1], lines[1])]) for a in range(4)]
 
+    coarse_coefficients(REACH, 0)
+
+    @pl.when(n == 0)
+    def _():
+        for _, receives, make, _ in transfers["first_trace"]:
+            when(receives, lambda make=make: make().wait_recv())
+        duo_begin[0] = begin[...]
+        interior(begin, duo_first.at[0])
+        finish_rate(duo_first.at[0], recv.at[0, 3], recv.at[1, 3])
+
+    duo_begin[1] = states[2]
+    duo_first[1] = rates[2]
+    duo_rates[0] = rates[...]
+    duo_rates[1] = jnp.zeros((3,) + FIELD, jnp.float32)
+
+    def duo_copy(k, d, slot):
+        return remote(
+            duo_send.at[k, slot],
+            duo_recv.at[1 - k, slot],
+            duo_out.at[k, slot],
+            duo_in.at[1 - k, slot],
+            (n, s + d),
+        )
+
+    def duo_launch(slot):
+        for k, d in enumerate((-1, 1)):
+            pl.when(has[d])(lambda k=k, d=d: duo_copy(k, d, slot).start())
+
+    def duo_await(slot):
+        for k, d in enumerate((-1, 1)):
+            pl.when(has[-d])(lambda k=k, d=d: duo_copy(k, d, slot).wait_recv())
+
+    def duo_fresh(target, factor, rate, slot, halo):
+        def outer(x, carry):
+            if halo is None:
+                lower, upper = rate(x)[0], rate(x)[3]
+            else:
+                lower, upper = finish_rate(rate(x), duo_recv.at[0, halo, x], duo_recv.at[1, halo, x])
+            first = duo_base[x, 0] + factor * lower
+            last = duo_base[x, 3] + factor * upper
+            target[x, 0] = first
+            target[x, 3] = last
+            pack(first, last, duo_send.at[0, slot, x], duo_send.at[1, slot, x])
+            return carry
+
+        def inner(x, carry):
+            target[x, 1:3] = duo_base[x, 1:3] + factor * rate(x)[1:3]
+            return carry
+
+        lax.fori_loop(0, 2, outer, 0)
+        duo_launch(slot)
+        lax.fori_loop(0, 2, inner, 0)
+
+    def opening(x, carry):
+        duo_base[x] = (
+            duo_begin[x]
+            - DT * duo_rates[x, 0]
+            + (H / 24.0) * (5.0 * duo_rates[x, 0] + 8.0 * duo_rates[x, 1] - duo_rates[x, 2])
+        )
+        return carry
+
+    lax.fori_loop(0, 2, opening, 0)
+    duo_fresh(duo_mid, DT, lambda x: duo_first.at[x], 0, None)
+    start("begin2")
+
+    def duo_closing(slot):
+        def prepare(x, carry):
+            duo_base[x] = (
+                duo_mid[x]
+                - DT * duo_rates[x, 1]
+                + (H / 24.0) * (8.0 * duo_rates[x, 1] + 5.0 * duo_rates[x, 2] - duo_rates[x, 0])
+            )
+            interior(duo_mid.at[x], duo_rates.at[x, 1])
+            return carry
+
+        lax.fori_loop(0, 2, prepare, 0)
+        duo_await(slot)
+        duo_fresh(duo_end, DT, lambda x: duo_rates.at[x, 1], slot + 1, slot)
+
+    def duo_middle(slot):
+        def prepare(x, carry):
+            duo_base[x] = duo_begin[x] + (H / 24.0) * (5.0 * duo_first[x] + 8.0 * duo_rates[x, 1])
+            interior(duo_end.at[x], duo_rates.at[x, 2])
+            return carry
+
+        lax.fori_loop(0, 2, prepare, 0)
+        duo_await(slot)
+        duo_fresh(duo_mid, -H / 24.0, lambda x: duo_rates.at[x, 2], slot + 1, slot)
+
+    duo_closing(0)
+    start("begin3")
+    for x in range(2):
+        duo_rates[x, 0] = duo_first[x]
+        old0[x, 1 : ROWS + 1] = restricted(duo_begin.at[x])
+    start("row0")
+    start("flow1")
+    duo_middle(1)
+    start("begin4")
+    duo_closing(2)
+    start("begin5")
+    start("flow2")
+    duo_middle(3)
+    start("begin6")
+    duo_closing(4)
+    for x in range(2):
+        old1[x, 1 : ROWS + 1] = restricted(duo_end.at[x])
+    start("row1")
+    start("begin7")
+
+    def last_rate(x, carry):
+        interior(duo_end.at[x], duo_rates.at[x, 2])
+        return carry
+
+    lax.fori_loop(0, 2, last_rate, 0)
+    arrive("row0")
+    low = MID - 1
+    h_rates0 = [advance(old0[x], low) - old0[x, 1 : ROWS + 1] for x in range(2)]
+    duo_await(5)
+    offsets = []
+    for x in range(2):
+        finish_rate(duo_rates.at[x, 2], duo_recv.at[0, 5, x], duo_recv.at[1, 5, x])
+    quadratures = [
+        restricted(
+            [
+                (H / 6.0) * (duo_first[x, a] + 4.0 * duo_rates[x, 1, a] + duo_rates[x, 2, a])
+                for a in range(4)
+            ]
+        )
+        for x in range(2)
+    ]
+    arrive("row1")
+    for x in (1, 0):
+        h_rate0 = h_rates0[x]
+        h_rate1 = advance(old1[x], low) - old1[x, 1 : ROWS + 1]
+        trapezoid = 0.5 * (h_rate0 + h_rate1)
+        offset = -h_rate0 + trapezoid + (quadratures[x] - trapezoid)
+        if x == 1:
+            leaving[...] = offset
+            start("hop")
+    is_first = n == 0
+    offset = offset + jnp.where(is_first, old0[0, 1 : ROWS + 1] + h_rates0[0], 0.0)
+
     arrive("begin_trace")
-    for _, receives, make, _ in transfers["first_trace"]:
-        when(receives, lambda make=make: make().wait_recv())
-    arrive("begin")
+    for piece in range(8):
+        arrive(f"begin{piece}")
     interior(begin, first_rate)
-    lower, upper = finish_rate(first_rate, 3)
+    lower, upper = finish_rate(first_rate, recv.at[0, 3], recv.at[1, 3])
 
     def fine_copy(k, d, slot):
         return remote(
@@ -570,14 +748,21 @@
         last = origin[3] + factor * upper
         u[0] = first
         u[3] = last
-        pack(first, last, slot)
-        launch(slot)
+        if slot is not None:
+            pack(first, last, send.at[0, slot], send.at[1, slot])
+            launch(slot)
         u[1:3] = origin[1:3] + factor * rate[1:3]
 
     base[...] = base[...] + begin[...]
     fresh(mid_state, base, DT, first_rate, lower, upper, 4)
-
-    def to_closing(slot):
+    start("flow3")
+
+    arrive("hop")
+    group[z, pl.ds(ROWS, ROWS)] = offset + passed[...]
+    start("group")
+    start("side0")
+
+    def to_closing(slot, out_slot):
         base[...] = (
             mid_state[...]
             - DT * rates[1]
@@ -585,64 +770,41 @@
         )
         interior(mid_state, rates.at[1])
         await_fine(slot)
-        lower, upper = finish_rate(rates.at[1], slot)
-        fresh(end_state, base, DT, rates.at[1], lower, upper, slot + 1)
-
-    start("flow1")
-    to_closing(4)
-    rates[0] = first_rate[...]
-
-    old0[1 : ROWS + 1] = restricted(begin)
-    start("row0")
-    start("flow2")
-
-    def sweep(index, carry):
-        slot = 5 + 2 * index
+        lower, upper = finish_rate(rates.at[1], recv.at[0, slot], recv.at[1, slot])
+        fresh(end_state, base, DT, rates.at[1], lower, upper, out_slot)
+
+    def to_middle(slot):
         base[...] = begin[...] + (H / 24.0) * (5.0 * first_rate[...] + 8.0 * rates[1])
         interior(end_state, rates.at[2])
         await_fine(slot)
-        lower, upper = finish_rate(rates.at[2], slot)
+        lower, upper = finish_rate(rates.at[2], recv.at[0, slot], recv.at[1, slot])
         fresh(mid_state, base, -H / 24.0, rates.at[2], lower, upper, slot + 1)
-        to_closing(slot + 1)
-        return carry
-
-    sweep(0, 0)
-    start("flow3")
-    sweep(1, 0)
-
-    old1[1 : ROWS + 1] = restricted(end_state)
-    start("row1")
-    interior(end_state, rates.at[2])
-    for name in ("flow1", "flow2", "flow3", "row0"):
+
+    to_closing(4, 5)
+    rates[0] = first_rate[...]
+    before0 = restricted(begin)
+
+    to_middle(5)
+    for shift in (1, 3, 2):
+        make = transfers["group"][shift - 1][2]
+        make().wait_recv()
+        start(f"side{shift}")
+    for name in ("flow1", "flow2", "flow3"):
         arrive(name)
-    lax.fori_loop(0, 2 * REACH + 1, coarse_coefficients, 0)
-    low = MID - 1
-    before0 = old0[1 : ROWS + 1]
-    h_rate0 = advance(old0[...], low) - before0
-    await_fine(9)
-    finish_rate(rates.at[2], 9)
-    quadrature = restricted(
-        [(H / 6.0) * (first_rate[a] + 4.0 * rates[1, a] + rates[2, a]) for a in range(4)]
-    )
-    arrive("row1")
-    before1 = old1[1 : ROWS + 1]
-    h_rate1 = advance(old1[...], low) - before1
-    trapezoid = 0.5 * (h_rate0 + h_rate1)
-    offset = -h_rate0 + trapezoid + (quadrature - trapezoid)
-    is_first = n == 0
-    offset = offset + jnp.where(is_first, before0 + h_rate0, 0.0)
-
-    group[z, pl.ds(ROWS, ROWS)] = offset
-    start("group")
-    arrive("group")
-    start("side")
-    arrive("side")
+    lax.fori_loop(0, REACH, coarse_coefficients, 0)
+    lax.fori_loop(REACH + 1, 2 * REACH + 1, coarse_coefficients, 0)
+    to_closing(6, 7)
+    for shift in range(GROUP):
+        arrive(f"side{shift}")
     y = group[0]
     y = advance(y, MID - 4) + group[1, 1:11]
     y = advance(y, MID - 3) + group[2, 2:10]
     y = advance(y, MID - 2)[1:5] + group[3, 4:8]
     partial[...] = y
     start("part")
+    to_middle(7)
+    to_closing(8, None)
+    before1 = restricted(end_state)
     arrive("part")
     y = far[...]
     for step in range(4):
@@ -673,8 +835,10 @@
     for name in transfers:
         sent(name)
     for k, d in enumerate((-1, 1)):
-        for slot in range(4, 10):
+        for slot in range(4, 9):
             pl.when(has[d])(lambda k=k, d=d, slot=slot: fine_copy(k, d, slot).wait_send())
+        for slot in range(6):
+            pl.when(has[d])(lambda k=k, d=d, slot=slot: duo_copy(k, d, slot).wait_send())
 
 
 def solution(mesh):
@@ -712,13 +876,23 @@
                 vmem(*FIELD),
                 vmem(*FIELD),
                 vmem(*FIELD),
-                vmem(2, 10, 2, 8, LANES),
-                vmem(2, 10, 2, 8, LANES),
+                vmem(2, 9, 2, 8, LANES),
+                vmem(2, 9, 2, 8, LANES),
+                vmem(2, *FIELD),
+                vmem(2, *FIELD),
+                vmem(2, 3, *FIELD),
+                vmem(2, *FIELD),
+                vmem(2, *FIELD),
+                vmem(2, *FIELD),
+                vmem(2, 6, 2, 2, 8, LANES),
+                vmem(2, 6, 2, 2, 8, LANES),
+                vmem(ROWS, 8, LANES),
+                vmem(ROWS, 8, LANES),
                 vmem(32, LANES),
                 vmem(2 * REACH + 1, ROWS, 3, 8, LANES),
                 vmem(7, 2 * REACH + 1, ROWS, 8, LANES),
-                vmem(ROWS + 2, 8, LANES),
-                vmem(ROWS + 2, 8, LANES),
+                vmem(2, ROWS + 2, 8, LANES),
+                vmem(2, ROWS + 2, 8, LANES),
                 vmem(GROUP, 3 * ROWS, 8, LANES),
                 vmem(ROWS, 8, LANES),
                 vmem(3 * ROWS, 8, LANES),
@@ -727,18 +901,22 @@
                 vmem(3, *FIELD),
                 dma(3),
                 dma(3),
-                dma(2, 10),
-                dma(2, 10),
+                dma(2, 9),
+                dma(2, 9),
+                dma(2, 6),
+                dma(2, 6),
                 pltpu.SemaphoreType.DMA,
                 pltpu.SemaphoreType.DMA,
+                dma(8),
+                dma(8),
                 dma(6),
                 dma(6),
                 dma(2, 2),
                 dma(2, 2),
                 dma(3),
                 dma(3),
-                dma(2),
-                dma(2),
+                dma(2, GROUP),
+                dma(2, GROUP),
                 dma(15),
                 dma(15),
             ],

time: 68.8 us -> 65.1 us (0.946)
  Pallas kernels: 66.8 us -> 63.1 us
    pallas_call x1, Pallas kernels: 66.8 us -> 63.1 us  [body(): pl.pallas_call(functools.partial(kernel, steps, columns), out_shape=jax.S...]
where the time goes in v4:
time: 65.1 us; the launch traced here: 64.9 us
  Pallas kernels  63.1 us (97%)
  local copies, waits for them, and re-layouts  1.77 us (3%)
    pallas_call x1, Pallas kernels, body(): pl.pallas_call(functools.partial(kernel, steps, columns), out_shape=jax.S...  63.1 us
    unnamed x1, local copies, waits for them, and re-layouts  1.77 us

profile of v4, /device:TPU:104, one launch (start us, length us, event | category | flops | bytes accessed | tf_op | source)
XLA Modules:
  0.0 64.9 jit_solution(3232557589578479278)
XLA Ops:
  0.0 63.1 %shard_map.37 = f32[3,4,4,2,8,128]{5,4,3,2,1,0:T(8,128)} custom-call(f32[3,4,4,2,8,128]{5,4,3,2,1,0:T(8,128)} %bitcast.5, f32[4,4,2,8,128]{4,3,2,1,0:T(8,128)} %bitcast.7, bf16[3,4,4,16,128]{4,3,2,1,0:T(8,128)(2,1)} %bitcast.6), custom_call_target="tpu_custom_call" | custom-call | tf_op jit(solution)/shard_map/pallas_call | solution.py:855
  63.1 1.8 %copy.5 = f32[1,3,64,4,128]{4,3,2,1,0:T(4,128)} copy(f32[1,3,64,4,128]{4,3,2,1,0:T(4,128)} %bitcast.4) | data formatting | bytes 786432

commit v5 on v4

--- a/solution.py
+++ b/solution.py
@@ -16,7 +16,7 @@
 DT = 0.5 * H
 LIFT = 6.0
 ROWS = 4
-REACH = 3
+REACH = 1
 SPAN = (2 * REACH + 1) * ROWS
 MID = REACH * ROWS
 FIELD = (4, 4, 2, 8, LANES)
@@ -99,8 +99,7 @@
     group,
     partial,
     near,
-    mid,
-    far,
+    ends,
     result,
     load_sem,
     store_sem,
@@ -225,18 +224,18 @@
                 ),
                 None,
             )
-        for shift in range(GROUP):
-            part_of = (z + GROUP - shift) % GROUP
+        for j in range(GROUP - 1):
+            rows = 3 - j
             add(
-                f"side{shift}",
+                f"side{j}",
                 has[d],
                 has[-d],
                 functools.partial(
                     remote,
-                    group.at[part_of, pl.ds(ROWS, ROWS)],
-                    group.at[part_of, pl.ds(2 * ROWS if d < 0 else 0, ROWS)],
-                    side_send.at[k, shift],
-                    side_recv.at[1 - k, shift],
+                    group.at[j, pl.ds(ROWS if d < 0 else 2 * ROWS - rows, rows)],
+                    group.at[j, pl.ds(2 * ROWS if d < 0 else ROWS - rows, rows)],
+                    side_send.at[k, j],
+                    side_recv.at[1 - k, j],
                     (n, s + d),
                 ),
                 None,
@@ -264,21 +263,21 @@
         functools.partial(remote, leaving, passed, hop_send, hop_recv, (n + 1, s)),
         None,
     )
-    for index, d in enumerate((-3, -2, -1, 1, 2, 3)):
-        needed = None if abs(d) == 1 else g >= abs(d)
+    for index, d in enumerate((-1, 1)):
+        edge = pl.ds(0 if d < 0 else 1, ROWS - 1)
         add(
-            f"flow{abs(d)}",
-            both(needed, inside(d)),
-            both(needed, inside(-d)),
+            "flow",
+            has[d],
+            has[-d],
             functools.partial(
                 remote,
-                flows.at[REACH],
-                flows.at[REACH - d],
+                flows.at[REACH, edge],
+                flows.at[REACH - d, edge],
                 flow_send.at[index],
                 flow_recv.at[index],
                 (n, s + d),
             ),
-            (n, s - d),
+            None,
         )
     for shift in (1, 2, 3):
         add(
@@ -295,24 +294,21 @@
             ),
             (g * GROUP + (z + GROUP - shift) % GROUP, s),
         )
-    slot = 0
-    for distance, buffer in ((3, far), (2, mid), (1, near)):
-        for d in range(-distance, distance + 1):
-            add(
-                "part",
-                both(g + distance < groups, inside(d)),
-                both(g >= distance, inside(-d)),
-                functools.partial(
-                    remote,
-                    partial,
-                    buffer.at[pl.ds((distance - d) * ROWS, ROWS)],
-                    part_send.at[slot],
-                    part_recv.at[slot],
-                    (n + distance * GROUP, s + d),
-                ),
-                (n - distance * GROUP, s - d),
-            )
-            slot += 1
+    for d in (-1, 0, 1):
+        add(
+            "part",
+            both(g < groups - 1, inside(d)),
+            both(g > 0, inside(-d)),
+            functools.partial(
+                remote,
+                partial,
+                near.at[pl.ds((1 - d) * ROWS, ROWS)],
+                part_send.at[d + 1],
+                part_recv.at[d + 1],
+                (n + GROUP, s + d),
+            ),
+            (n - GROUP, s - d),
+        )
 
     def start(name):
         for sends, _, make, _ in transfers[name]:
@@ -343,8 +339,6 @@
     old1[...] = jnp.zeros(old1.shape, jnp.float32)
     group[...] = jnp.zeros(group.shape, jnp.float32)
     near[...] = jnp.zeros(near.shape, jnp.float32)
-    mid[...] = jnp.zeros(mid.shape, jnp.float32)
-    far[...] = jnp.zeros(far.shape, jnp.float32)
 
     barrier = pltpu.get_barrier_semaphore()
     expected = jnp.int32(0)
@@ -358,7 +352,7 @@
     for d in (-1, 1):
         greet(has[d], (n, s + d))
         expected = expected + has[d].astype(jnp.int32)
-    for name in ("begin_trace", "begin0", "flow2", "flow3", "group", "part"):
+    for name in ("begin_trace", "begin0", "group", "part"):
         for sends, receives, _, partner in transfers[name]:
             greet(receives, partner)
             expected = expected + (1 if sends is None else sends.astype(jnp.int32))
@@ -673,12 +667,11 @@
         duo_rates[x, 0] = duo_first[x]
         old0[x, 1 : ROWS + 1] = restricted(duo_begin.at[x])
     start("row0")
-    start("flow1")
+    start("flow")
     duo_middle(1)
     start("begin4")
     duo_closing(2)
     start("begin5")
-    start("flow2")
     duo_middle(3)
     start("begin6")
     duo_closing(4)
@@ -755,12 +748,10 @@
 
     base[...] = base[...] + begin[...]
     fresh(mid_state, base, DT, first_rate, lower, upper, 4)
-    start("flow3")
 
     arrive("hop")
     group[z, pl.ds(ROWS, ROWS)] = offset + passed[...]
     start("group")
-    start("side0")
 
     def to_closing(slot, out_slot):
         base[...] = (
@@ -785,40 +776,50 @@
     before0 = restricted(begin)
 
     to_middle(5)
-    for shift in (1, 3, 2):
-        make = transfers["group"][shift - 1][2]
-        make().wait_recv()
-        start(f"side{shift}")
-    for name in ("flow1", "flow2", "flow3"):
-        arrive(name)
-    lax.fori_loop(0, REACH, coarse_coefficients, 0)
-    lax.fori_loop(REACH + 1, 2 * REACH + 1, coarse_coefficients, 0)
+    arrive("flow")
+    coarse_coefficients(REACH - 1, 0)
+    coarse_coefficients(REACH + 1, 0)
+    for j in range(GROUP):
+
+        @pl.when(z != j)
+        def _():
+            remote(
+                group.at[j, pl.ds(ROWS, ROWS)],
+                group.at[j, pl.ds(ROWS, ROWS)],
+                group_send.at[0],
+                group_recv.at[(z + GROUP - 1 - j) % GROUP],
+                (n, s),
+            ).wait_recv()
+
+        if j < GROUP - 1:
+            start(f"side{j}")
     to_closing(6, 7)
-    for shift in range(GROUP):
-        arrive(f"side{shift}")
-    y = group[0]
-    y = advance(y, MID - 4) + group[1, 1:11]
-    y = advance(y, MID - 3) + group[2, 2:10]
-    y = advance(y, MID - 2)[1:5] + group[3, 4:8]
-    partial[...] = y
-    start("part")
+
+    def coarse_chain():
+        arrive("part")
+        y = near[...]
+        line = [y[4:8]]
+        for j in range(GROUP):
+            y = advance(y, j) + group[j, j + 1 : 11 - j]
+            line.append(y[3 - j : 7 - j])
+        partial[...] = y
+        start("part")
+        begin_rows, finish = line[0], line[1]
+        for j in range(1, GROUP):
+            begin_rows = jnp.where(z == j, line[j], begin_rows)
+            finish = jnp.where(z == j, line[j + 1], finish)
+        ends[0] = begin_rows
+        ends[1] = finish
+
+    for j in range(GROUP - 1):
+        arrive(f"side{j}")
+    pl.when(g == 0)(coarse_chain)
     to_middle(7)
     to_closing(8, None)
     before1 = restricted(end_state)
-    arrive("part")
-    y = far[...]
-    for step in range(4):
-        y = advance(y, step)
-    y = y + mid[...]
-    for step in range(4, 8):
-        y = advance(y, step)
-    y = y + near[...]
-    for j in range(3):
-        count = 12 - 2 * j
-        stepped = advance(y, MID - 4 + j) + group[j, j + 1 : 11 - j]
-        y = jnp.where(z > j, stepped, y[1 : count - 1])
-    finish = advance(y, MID - 1) + group[z, pl.ds(ROWS, ROWS)]
-    begin_rows = jnp.where(is_first, before0, y[1:5])
+    pl.when(g > 0)(coarse_chain)
+    begin_rows = jnp.where(is_first, before0, ends[0])
+    finish = ends[1]
     delta0 = begin_rows - before0
     delta1 = finish - before1
 
@@ -896,8 +897,7 @@
                 vmem(GROUP, 3 * ROWS, 8, LANES),
                 vmem(ROWS, 8, LANES),
                 vmem(3 * ROWS, 8, LANES),
-                vmem(5 * ROWS, 8, LANES),
-                vmem(7 * ROWS, 8, LANES),
+                vmem(2, ROWS, 8, LANES),
                 vmem(3, *FIELD),
                 dma(3),
                 dma(3),
@@ -909,16 +909,16 @@
                 pltpu.SemaphoreType.DMA,
                 dma(8),
                 dma(8),
-                dma(6),
-                dma(6),
+                dma(2),
+                dma(2),
                 dma(2, 2),
                 dma(2, 2),
                 dma(3),
                 dma(3),
                 dma(2, GROUP),
                 dma(2, GROUP),
-                dma(15),
-                dma(15),
+                dma(3),
+                dma(3),
             ],
             compiler_params=pltpu.CompilerParams(
                 collective_id=0, has_side_effects=True, vmem_limit_bytes=60 * 1024 * 1024

time: 65.1 us -> 70.1 us (1.077)
  the two profiles are of different devices: /device:TPU:104 before, /device:TPU:31 now
where the time goes in v5:
time: 70.1 us; the launch traced here: 69.9 us
  Pallas kernels  68.2 us (97%)
  local copies, waits for them, and re-layouts  1.77 us (3%)
    pallas_call x1, Pallas kernels, body(): pl.pallas_call(functools.partial(kernel, steps, columns), out_shape=jax.S...  68.2 us
    unnamed x1, local copies, waits for them, and re-layouts  1.77 us

profile of v5, /device:TPU:31, one launch (start us, length us, event | category | flops | bytes accessed | tf_op | source)
XLA Modules:
  0.0 69.9 jit_solution(4911900735010193846)
XLA Ops:
  0.0 68.2 %shard_map.37 = f32[3,4,4,2,8,128]{5,4,3,2,1,0:T(8,128)} custom-call(f32[3,4,4,2,8,128]{5,4,3,2,1,0:T(8,128)} %bitcast.5, f32[4,4,2,8,128]{4,3,2,1,0:T(8,128)} %bitcast.7, bf16[3,4,4,16,128]{4,3,2,1,0:T(8,128)(2,1)} %bitcast.6), custom_call_target="tpu_custom_call" | custom-call | tf_op jit(solution)/shard_map/pallas_call | solution.py:856
  68.2 1.8 %copy.5 = f32[1,3,64,4,128]{4,3,2,1,0:T(4,128)} copy(f32[1,3,64,4,128]{4,3,2,1,0:T(4,128)} %bitcast.4) | data formatting | bytes 786432

commit v6 on v4

--- a/solution.py
+++ b/solution.py
@@ -225,18 +225,18 @@
                 ),
                 None,
             )
-        for shift in range(GROUP):
-            part_of = (z + GROUP - shift) % GROUP
+        for j in range(GROUP - 1):
+            rows = 3 - j
             add(
-                f"side{shift}",
+                f"side{j}",
                 has[d],
                 has[-d],
                 functools.partial(
                     remote,
-                    group.at[part_of, pl.ds(ROWS, ROWS)],
-                    group.at[part_of, pl.ds(2 * ROWS if d < 0 else 0, ROWS)],
-                    side_send.at[k, shift],
-                    side_recv.at[1 - k, shift],
+                    group.at[j, pl.ds(ROWS if d < 0 else 2 * ROWS - rows, rows)],
+                    group.at[j, pl.ds(2 * ROWS if d < 0 else ROWS - rows, rows)],
+                    side_send.at[k, j],
+                    side_recv.at[1 - k, j],
                     (n, s + d),
                 ),
                 None,
@@ -407,6 +407,7 @@
     start("states")
     start("begin0")
     start("begin1")
+    start("begin2")
 
     load_wind.wait()
     for axis in range(3):
@@ -447,42 +448,33 @@
 
     def interior(u, out):
         for b in range(4):
-            ub = u[:, b]
-            turned = pltpu.roll(ub, 4, 2)
-            along_x = jnp.stack([weighted([(DER[a, c], ub[c]) for c in range(4)]) for a in range(4)])
-            along_y = weighted([(DER[b, c], ub if c == b else u[:, c]) for c in range(4)])
-            along_z = jnp.stack(
-                [
-                    same[i][0] * ub[:, 0]
-                    + cross[i][0] * turned[:, 0]
-                    + same[i][1] * ub[:, 1]
-                    + cross[i][1] * turned[:, 1]
-                    for i in range(2)
-                ],
-                axis=1,
-            )
-            total = (
-                nv[0, :, b] * along_x
-                + nv[1, :, b] * along_y
-                + nv[2, :, b] * along_z
-                + diag[:, b] * ub
-            )
-            faces = jnp.stack(
-                [
-                    zl[:, b] * pltpu.roll(turned[:, 1], 1, 2),
-                    zh[:, b] * pltpu.roll(turned[:, 0], LANES - 1, 2),
-                ],
-                axis=1,
-            )
-            total = total + faces
-            if b == 0:
-                total = total + yl[...] * pltpu.roll(u[:, 3], CZ, 3)
-            if b == 3:
-                total = total + yh[...] * pltpu.roll(u[:, 0], LANES - CZ, 3)
-            out[0, b] = total[0] + xli[b] * pltpu.roll(ub[3], 1, 1)
-            out[1, b] = total[1]
-            out[2, b] = total[2]
-            out[3, b] = total[3] + xhi[b] * pltpu.roll(ub[0], 7, 1)
+            pair = [u[:, b, 0], u[:, b, 1]]
+            turned = [pltpu.roll(half, 4, 1) for half in pair]
+            for i in range(2):
+                own = pair[i]
+                along_z = (
+                    same[i][0] * pair[0]
+                    + cross[i][0] * turned[0]
+                    + same[i][1] * pair[1]
+                    + cross[i][1] * turned[1]
+                )
+                total = diag[:, b, i] * own + nv[2, :, b, i] * along_z
+                if i == 0:
+                    total = total + zl[:, b] * pltpu.roll(turned[1], 1, 2)
+                else:
+                    total = total + zh[:, b] * pltpu.roll(turned[0], LANES - 1, 2)
+                others = [own if c == b else u[:, c, i] for c in range(4)]
+                along_y = weighted([(DER[b, c], others[c]) for c in range(4)])
+                total = total + nv[1, :, b, i] * along_y
+                if b == 0:
+                    total = total + yl[:, i] * pltpu.roll(others[3], CZ, 2)
+                if b == 3:
+                    total = total + yh[:, i] * pltpu.roll(others[0], LANES - CZ, 2)
+                along_x = jnp.stack([weighted([(DER[a, c], own[c]) for c in range(4)]) for a in range(4)])
+                total = total + nv[0, :, b, i] * along_x
+                out[0, b, i] = total[0] + xli[b, i] * pltpu.roll(own[3], 1, 0)
+                out[1:3, b, i] = total[1:3]
+                out[3, b, i] = total[3] + xhi[b, i] * pltpu.roll(own[0], 7, 0)
 
     def finish_rate(out, low_from, high_from):
         low, high = unpack(low_from, high_from)
@@ -641,7 +633,7 @@
 
     lax.fori_loop(0, 2, opening, 0)
     duo_fresh(duo_mid, DT, lambda x: duo_first.at[x], 0, None)
-    start("begin2")
+    start("begin3")
 
     def duo_closing(slot):
         def prepare(x, carry):
@@ -668,24 +660,22 @@
         duo_fresh(duo_mid, -H / 24.0, lambda x: duo_rates.at[x, 2], slot + 1, slot)
 
     duo_closing(0)
-    start("begin3")
+    start("begin4")
     for x in range(2):
         duo_rates[x, 0] = duo_first[x]
         old0[x, 1 : ROWS + 1] = restricted(duo_begin.at[x])
     start("row0")
     start("flow1")
     duo_middle(1)
-    start("begin4")
+    start("begin5")
     duo_closing(2)
-    start("begin5")
-    start("flow2")
+    start("begin6")
     duo_middle(3)
-    start("begin6")
+    start("begin7")
     duo_closing(4)
     for x in range(2):
         old1[x, 1 : ROWS + 1] = restricted(duo_end.at[x])
     start("row1")
-    start("begin7")
 
     def last_rate(x, carry):
         interior(duo_end.at[x], duo_rates.at[x, 2])
@@ -755,12 +745,11 @@
 
     base[...] = base[...] + begin[...]
     fresh(mid_state, base, DT, first_rate, lower, upper, 4)
-    start("flow3")
 
     arrive("hop")
     group[z, pl.ds(ROWS, ROWS)] = offset + passed[...]
     start("group")
-    start("side0")
+    start("flow2")
 
     def to_closing(slot, out_slot):
         base[...] = (
@@ -785,17 +774,27 @@
     before0 = restricted(begin)
 
     to_middle(5)
-    for shift in (1, 3, 2):
-        make = transfers["group"][shift - 1][2]
-        make().wait_recv()
-        start(f"side{shift}")
-    for name in ("flow1", "flow2", "flow3"):
-        arrive(name)
-    lax.fori_loop(0, REACH, coarse_coefficients, 0)
-    lax.fori_loop(REACH + 1, 2 * REACH + 1, coarse_coefficients, 0)
+    for j in range(GROUP):
+
+        @pl.when(z != j)
+        def _():
+            remote(
+                group.at[j, pl.ds(ROWS, ROWS)],
+                group.at[j, pl.ds(ROWS, ROWS)],
+                group_send.at[0],
+                group_recv.at[(z + GROUP - 1 - j) % GROUP],
+                (n, s),
+            ).wait_recv()
+
+        if j < GROUP - 1:
+            start(f"side{j}")
+    start("flow3")
+    arrive("flow1")
+    coarse_coefficients(REACH - 1, 0)
+    coarse_coefficients(REACH + 1, 0)
     to_closing(6, 7)
-    for shift in range(GROUP):
-        arrive(f"side{shift}")
+    for j in range(GROUP - 1):
+        arrive(f"side{j}")
     y = group[0]
     y = advance(y, MID - 4) + group[1, 1:11]
     y = advance(y, MID - 3) + group[2, 2:10]
@@ -805,6 +804,10 @@
     to_middle(7)
     to_closing(8, None)
     before1 = restricted(end_state)
+    arrive("flow2")
+    arrive("flow3")
+    lax.fori_loop(0, REACH - 1, coarse_coefficients, 0)
+    lax.fori_loop(REACH + 2, 2 * REACH + 1, coarse_coefficients, 0)
     arrive("part")
     y = far[...]
     for step in range(4):

time: 65.1 us -> 66.7 us (1.025)
  the two profiles are of different devices: /device:TPU:104 before, /device:TPU:56 now
where the time goes in v6:
time: 66.7 us; the launch traced here: 66.5 us
  Pallas kernels  64.7 us (97%)
  local copies, waits for them, and re-layouts  1.77 us (3%)
    pallas_call x1, Pallas kernels, body(): pl.pallas_call(functools.partial(kernel, steps, columns), out_shape=jax.S...  64.7 us
    unnamed x1, local copies, waits for them, and re-layouts  1.77 us

profile of v6, /device:TPU:56, one launch (start us, length us, event | category | flops | bytes accessed | tf_op | source)
XLA Modules:
  0.0 66.5 jit_solution(9452263554689430891)
XLA Ops:
  0.0 64.7 %shard_map.37 = f32[3,4,4,2,8,128]{5,4,3,2,1,0:T(8,128)} custom-call(f32[3,4,4,2,8,128]{5,4,3,2,1,0:T(8,128)} %bitcast.5, f32[4,4,2,8,128]{4,3,2,1,0:T(8,128)} %bitcast.7, bf16[3,4,4,16,128]{4,3,2,1,0:T(8,128)(2,1)} %bitcast.6), custom_call_target="tpu_custom_call" | custom-call | tf_op jit(solution)/shard_map/pallas_call | solution.py:858
  64.7 1.8 %copy.5 = f32[1,3,64,4,128]{4,3,2,1,0:T(4,128)} copy(f32[1,3,64,4,128]{4,3,2,1,0:T(4,128)} %bitcast.4) | data formatting | bytes 786432

commit v7 on v6

--- a/solution.py
+++ b/solution.py
@@ -60,7 +60,8 @@
     states_hbm,
     start_hbm,
     wind_hbm,
-    out_hbm,
+    fields_hbm,
+    lifted_hbm,
     states,
     wind,
     begin,
@@ -241,22 +242,19 @@
                 ),
                 None,
             )
-    for piece in range(8):
-        where_to = (piece // 2, pl.ds(2 * (piece % 2), 2))
-        add(
-            f"begin{piece}",
-            n < steps - 1,
-            n > 0,
-            functools.partial(
-                remote,
-                states_hbm.at[(2,) + where_to],
-                begin.at[where_to],
-                begin_send.at[piece],
-                begin_recv.at[piece],
-                (n + 1, s),
-            ),
-            (n - 1, s),
-        )
+    def begin_copy(piece):
+        where_to = (piece // 4, piece % 4)
+        return remote(
+            states_hbm.at[(2,) + where_to],
+            begin.at[where_to],
+            begin_send.at[piece],
+            begin_recv.at[piece],
+            (n + 1, s),
+        )
+
+    def begin_start(piece):
+        pl.when(n < steps - 1)(lambda: begin_copy(piece).start())
+
     add(
         "hop",
         n < steps - 1,
@@ -358,7 +356,9 @@
     for d in (-1, 1):
         greet(has[d], (n, s + d))
         expected = expected + has[d].astype(jnp.int32)
-    for name in ("begin_trace", "begin0", "flow2", "flow3", "group", "part"):
+    greet(n > 0, (n - 1, s))
+    expected = expected + (n < steps - 1).astype(jnp.int32)
+    for name in ("begin_trace", "flow2", "flow3", "group", "part"):
         for sends, receives, _, partner in transfers[name]:
             greet(receives, partner)
             expected = expected + (1 if sends is None else sends.astype(jnp.int32))
@@ -405,9 +405,8 @@
     start("begin_trace")
     start("first_trace")
     start("states")
-    start("begin0")
-    start("begin1")
-    start("begin2")
+    for piece in range(4):
+        begin_start(piece)
 
     load_wind.wait()
     for axis in range(3):
@@ -633,10 +632,10 @@
 
     lax.fori_loop(0, 2, opening, 0)
     duo_fresh(duo_mid, DT, lambda x: duo_first.at[x], 0, None)
-    start("begin3")
 
     def duo_closing(slot):
         def prepare(x, carry):
+            begin_start(4 + 2 * slot + x)
             duo_base[x] = (
                 duo_mid[x]
                 - DT * duo_rates[x, 1]
@@ -651,6 +650,7 @@
 
     def duo_middle(slot):
         def prepare(x, carry):
+            begin_start(4 + 2 * slot + x)
             duo_base[x] = duo_begin[x] + (H / 24.0) * (5.0 * duo_first[x] + 8.0 * duo_rates[x, 1])
             interior(duo_end.at[x], duo_rates.at[x, 2])
             return carry
@@ -660,24 +660,21 @@
         duo_fresh(duo_mid, -H / 24.0, lambda x: duo_rates.at[x, 2], slot + 1, slot)
 
     duo_closing(0)
-    start("begin4")
     for x in range(2):
         duo_rates[x, 0] = duo_first[x]
         old0[x, 1 : ROWS + 1] = restricted(duo_begin.at[x])
     start("row0")
     start("flow1")
     duo_middle(1)
-    start("begin5")
     duo_closing(2)
-    start("begin6")
     duo_middle(3)
-    start("begin7")
     duo_closing(4)
     for x in range(2):
         old1[x, 1 : ROWS + 1] = restricted(duo_end.at[x])
     start("row1")
 
     def last_rate(x, carry):
+        begin_start(14 + x)
         interior(duo_end.at[x], duo_rates.at[x, 2])
         return carry
 
@@ -711,8 +708,8 @@
     offset = offset + jnp.where(is_first, old0[0, 1 : ROWS + 1] + h_rates0[0], 0.0)
 
     arrive("begin_trace")
-    for piece in range(8):
-        arrive(f"begin{piece}")
+    for piece in range(16):
+        pl.when(n > 0)(lambda piece=piece: begin_copy(piece).wait_recv())
     interior(begin, first_rate)
     lower, upper = finish_rate(first_rate, recv.at[0, 3], recv.at[1, 3])
 
@@ -803,6 +800,12 @@
     start("part")
     to_middle(7)
     to_closing(8, None)
+    stores = [
+        pltpu.make_async_copy(field, fields_hbm.at[index], store_sem.at[3 + index])
+        for index, field in enumerate((begin, mid_state, end_state))
+    ]
+    for store in stores:
+        store.start()
     before1 = restricted(end_state)
     arrive("flow2")
     arrive("flow3")
@@ -825,18 +828,20 @@
     delta0 = begin_rows - before0
     delta1 = finish - before1
 
-    for index, (delta, field) in enumerate(
-        ((delta0, begin), (0.5 * (delta0 + delta1), mid_state), (delta1, end_state))
-    ):
+    for index, delta in enumerate((delta0, 0.5 * (delta0 + delta1), delta1)):
         lifted = prolonged(delta)
         for a in range(4):
-            result[index, a] = field[a] + lifted[a]
-        pltpu.make_async_copy(result.at[index], out_hbm.at[index], store_sem.at[index]).start()
+            result[index, a] = lifted[a]
+        pltpu.make_async_copy(result.at[index], lifted_hbm.at[index], store_sem.at[index]).start()
     for index in range(3):
-        pltpu.make_async_copy(result.at[index], out_hbm.at[index], store_sem.at[index]).wait()
+        pltpu.make_async_copy(result.at[index], lifted_hbm.at[index], store_sem.at[index]).wait()
+    for store in stores:
+        store.wait()
 
     for name in transfers:
         sent(name)
+    for piece in range(16):
+        pl.when(n < steps - 1)(lambda piece=piece: begin_copy(piece).wait_send())
     for k, d in enumerate((-1, 1)):
         for slot in range(4, 9):
             pl.when(has[d])(lambda k=k, d=d, slot=slot: fine_copy(k, d, slot).wait_send())
@@ -855,11 +860,11 @@
         f32 = jnp.float32
         vmem = lambda *shape: pltpu.VMEM(shape, f32)
         dma = lambda *shape: pltpu.SemaphoreType.DMA(shape)
-        out = pl.pallas_call(
+        fields, lifted = pl.pallas_call(
             functools.partial(kernel, steps, columns),
-            out_shape=jax.ShapeDtypeStruct((3,) + FIELD, f32),
+            out_shape=[jax.ShapeDtypeStruct((3,) + FIELD, f32)] * 2,
             in_specs=[pl.BlockSpec(memory_space=pltpu.HBM)] * 3,
-            out_specs=pl.BlockSpec(memory_space=pl.ANY),
+            out_specs=[pl.BlockSpec(memory_space=pl.ANY)] * 2,
             scratch_shapes=[
                 vmem(3, *FIELD),
                 pltpu.VMEM((3, 4, 4, 16, LANES), jnp.bfloat16),
@@ -903,15 +908,15 @@
                 vmem(7 * ROWS, 8, LANES),
                 vmem(3, *FIELD),
                 dma(3),
-                dma(3),
+                dma(6),
                 dma(2, 9),
                 dma(2, 9),
                 dma(2, 6),
                 dma(2, 6),
                 pltpu.SemaphoreType.DMA,
                 pltpu.SemaphoreType.DMA,
-                dma(8),
-                dma(8),
+                dma(16),
+                dma(16),
                 dma(6),
                 dma(6),
                 dma(2, 2),
@@ -927,7 +932,7 @@
                 collective_id=0, has_side_effects=True, vmem_limit_bytes=60 * 1024 * 1024
             ),
         )(states, first, wind)
-        return out.reshape(1, 3, 64, ROWS, LANES)
+        return (fields + lifted).reshape(1, 3, 64, ROWS, LANES)
 
     return jax.shard_map(
         body,

time: 66.7 us -> 65 us (0.975)
  the two profiles are of different devices: /device:TPU:56 before, /device:TPU:104 now
where the time goes in v7:
time: 65 us; the launch traced here: 64.8 us
  Pallas kernels  62.8 us (97%)
  other arithmetic  1.91 us (3%)
    pallas_call x1, Pallas kernels, body(): pl.pallas_call(functools.partial(kernel, steps, columns), out_shape=[jax....  62.8 us
    add x1, other arithmetic, body(): return (fields + lifted).reshape(1, 3, 64, ROWS, LANES)  1.91 us

profile of v7, /device:TPU:104, one launch (start us, length us, event | category | flops | bytes accessed | tf_op | source)
XLA Modules:
  0.0 64.8 jit_solution(3946491519300930474)
XLA Ops:
  0.0 62.8 %shard_map.37 = (f32[3,4,4,2,8,128]{5,4,3,2,1,0:T(8,128)}, f32[3,4,4,2,8,128]{5,4,3,2,1,0:T(8,128)}) custom-call(f32[3,4,4,2,8,128]{5,4,3,2,1,0:T(8,128)} %bitcast.4, f32[4,4,2,8,128]{4,3,2,1,0:T(8,128)} %bitcast.6, bf16[3,4,4,16,128]{4,3,2,1,0:T(8,128)(2,1)} %bitcast.5), custom_call_target="tpu_custom_call" | custom-call | tf_op jit(solution)/shard_map/pallas_call | solution.py:863
  62.8 1.9 %add.3 = f32[3,4,4,2,8,128]{5,4,3,2,1,0:T(8,128)} add(f32[3,4,4,2,8,128]{5,4,3,2,1,0:T(8,128)} %get-tuple-element.7, f32[3,4,4,2,8,128]{5,4,3,2,1,0:T(8,128)} %get-tuple-element.8) | non-fusion elementwise | flops 98304 | bytes 1179648 | tf_op jit(solution)/shard_map/add | solution.py:935

commit v8 on v7

--- a/solution.py
+++ b/solution.py
@@ -242,19 +242,13 @@
                 ),
                 None,
             )
-    def begin_copy(piece):
-        where_to = (piece // 4, piece % 4)
-        return remote(
-            states_hbm.at[(2,) + where_to],
-            begin.at[where_to],
-            begin_send.at[piece],
-            begin_recv.at[piece],
-            (n + 1, s),
-        )
-
-    def begin_start(piece):
-        pl.when(n < steps - 1)(lambda: begin_copy(piece).start())
-
+    add(
+        "begin",
+        n < steps - 1,
+        n > 0,
+        functools.partial(remote, states_hbm.at[2], begin, begin_send, begin_recv, (n + 1, s)),
+        (n - 1, s),
+    )
     add(
         "hop",
         n < steps - 1,
@@ -356,9 +350,7 @@
     for d in (-1, 1):
         greet(has[d], (n, s + d))
         expected = expected + has[d].astype(jnp.int32)
-    greet(n > 0, (n - 1, s))
-    expected = expected + (n < steps - 1).astype(jnp.int32)
-    for name in ("begin_trace", "flow2", "flow3", "group", "part"):
+    for name in ("begin_trace", "begin", "flow2", "flow3", "group", "part"):
         for sends, receives, _, partner in transfers[name]:
             greet(receives, partner)
             expected = expected + (1 if sends is None else sends.astype(jnp.int32))
@@ -405,8 +397,7 @@
     start("begin_trace")
     start("first_trace")
     start("states")
-    for piece in range(4):
-        begin_start(piece)
+    start("begin")
 
     load_wind.wait()
     for axis in range(3):
@@ -635,7 +626,6 @@
 
     def duo_closing(slot):
         def prepare(x, carry):
-            begin_start(4 + 2 * slot + x)
             duo_base[x] = (
                 duo_mid[x]
                 - DT * duo_rates[x, 1]
@@ -650,7 +640,6 @@
 
     def duo_middle(slot):
         def prepare(x, carry):
-            begin_start(4 + 2 * slot + x)
             duo_base[x] = duo_begin[x] + (H / 24.0) * (5.0 * duo_first[x] + 8.0 * duo_rates[x, 1])
             interior(duo_end.at[x], duo_rates.at[x, 2])
             return carry
@@ -658,6 +647,51 @@
         lax.fori_loop(0, 2, prepare, 0)
         duo_await(slot)
         duo_fresh(duo_mid, -H / 24.0, lambda x: duo_rates.at[x, 2], slot + 1, slot)
+
+    def fine_copy(k, d, slot):
+        return remote(
+            send.at[k, slot],
+            recv.at[1 - k, slot],
+            fine_send.at[k, slot],
+            fine_recv.at[1 - k, slot],
+            (n, s + d),
+        )
+
+    def launch(slot):
+        for k, d in enumerate((-1, 1)):
+            pl.when(has[d])(lambda k=k, d=d: fine_copy(k, d, slot).start())
+
+    def await_fine(slot):
+        for k, d in enumerate((-1, 1)):
+            pl.when(has[-d])(lambda k=k, d=d: fine_copy(k, d, slot).wait_recv())
+
+    def fresh(u, origin, factor, rate, lower, upper, slot):
+        first = origin[0] + factor * lower
+        last = origin[3] + factor * upper
+        u[0] = first
+        u[3] = last
+        if slot is not None:
+            pack(first, last, send.at[0, slot], send.at[1, slot])
+            launch(slot)
+        u[1:3] = origin[1:3] + factor * rate[1:3]
+
+    def to_closing(slot, out_slot):
+        base[...] = (
+            mid_state[...]
+            - DT * rates[1]
+            + (H / 24.0) * (8.0 * rates[1] + 5.0 * rates[2] - rates[0])
+        )
+        interior(mid_state, rates.at[1])
+        await_fine(slot)
+        lower, upper = finish_rate(rates.at[1], recv.at[0, slot], recv.at[1, slot])
+        fresh(end_state, base, DT, rates.at[1], lower, upper, out_slot)
+
+    def to_middle(slot):
+        base[...] = begin[...] + (H / 24.0) * (5.0 * first_rate[...] + 8.0 * rates[1])
+        interior(end_state, rates.at[2])
+        await_fine(slot)
+        lower, upper = finish_rate(rates.at[2], recv.at[0, slot], recv.at[1, slot])
+        fresh(mid_state, base, -H / 24.0, rates.at[2], lower, upper, slot + 1)
 
     duo_closing(0)
     for x in range(2):
@@ -667,14 +701,25 @@
     start("flow1")
     duo_middle(1)
     duo_closing(2)
+
+    arrive("begin_trace")
+    arrive("begin")
+    interior(begin, first_rate)
+    lower, upper = finish_rate(first_rate, recv.at[0, 3], recv.at[1, 3])
+
+    base[...] = base[...] + begin[...]
+    fresh(mid_state, base, DT, first_rate, lower, upper, 4)
+
     duo_middle(3)
+    to_closing(4, 5)
+    rates[0] = first_rate[...]
     duo_closing(4)
     for x in range(2):
         old1[x, 1 : ROWS + 1] = restricted(duo_end.at[x])
     start("row1")
+    to_middle(5)
 
     def last_rate(x, carry):
-        begin_start(14 + x)
         interior(duo_end.at[x], duo_rates.at[x, 2])
         return carry
 
@@ -707,70 +752,13 @@
     is_first = n == 0
     offset = offset + jnp.where(is_first, old0[0, 1 : ROWS + 1] + h_rates0[0], 0.0)
 
-    arrive("begin_trace")
-    for piece in range(16):
-        pl.when(n > 0)(lambda piece=piece: begin_copy(piece).wait_recv())
-    interior(begin, first_rate)
-    lower, upper = finish_rate(first_rate, recv.at[0, 3], recv.at[1, 3])
-
-    def fine_copy(k, d, slot):
-        return remote(
-            send.at[k, slot],
-            recv.at[1 - k, slot],
-            fine_send.at[k, slot],
-            fine_recv.at[1 - k, slot],
-            (n, s + d),
-        )
-
-    def launch(slot):
-        for k, d in enumerate((-1, 1)):
-            pl.when(has[d])(lambda k=k, d=d: fine_copy(k, d, slot).start())
-
-    def await_fine(slot):
-        for k, d in enumerate((-1, 1)):
-            pl.when(has[-d])(lambda k=k, d=d: fine_copy(k, d, slot).wait_recv())
-
-    def fresh(u, origin, factor, rate, lower, upper, slot):
-        first = origin[0] + factor * lower
-        last = origin[3] + factor * upper
-        u[0] = first
-        u[3] = last
-        if slot is not None:
-            pack(first, last, send.at[0, slot], send.at[1, slot])
-            launch(slot)
-        u[1:3] = origin[1:3] + factor * rate[1:3]
-
-    base[...] = base[...] + begin[...]
-    fresh(mid_state, base, DT, first_rate, lower, upper, 4)
-
+    to_closing(6, 7)
     arrive("hop")
     group[z, pl.ds(ROWS, ROWS)] = offset + passed[...]
     start("group")
     start("flow2")
 
-    def to_closing(slot, out_slot):
-        base[...] = (
-            mid_state[...]
-            - DT * rates[1]
-            + (H / 24.0) * (8.0 * rates[1] + 5.0 * rates[2] - rates[0])
-        )
-        interior(mid_state, rates.at[1])
-        await_fine(slot)
-        lower, upper = finish_rate(rates.at[1], recv.at[0, slot], recv.at[1, slot])
-        fresh(end_state, base, DT, rates.at[1], lower, upper, out_slot)
-
-    def to_middle(slot):
-        base[...] = begin[...] + (H / 24.0) * (5.0 * first_rate[...] + 8.0 * rates[1])
-        interior(end_state, rates.at[2])
-        await_fine(slot)
-        lower, upper = finish_rate(rates.at[2], recv.at[0, slot], recv.at[1, slot])
-        fresh(mid_state, base, -H / 24.0, rates.at[2], lower, upper, slot + 1)
-
-    to_closing(4, 5)
-    rates[0] = first_rate[...]
-    before0 = restricted(begin)
-
-    to_middle(5)
+    to_middle(7)
     for j in range(GROUP):
 
         @pl.when(z != j)
@@ -789,7 +777,15 @@
     arrive("flow1")
     coarse_coefficients(REACH - 1, 0)
     coarse_coefficients(REACH + 1, 0)
-    to_closing(6, 7)
+    to_closing(8, None)
+    stores = [
+        pltpu.make_async_copy(field, fields_hbm.at[index], store_sem.at[3 + index])
+        for index, field in enumerate((begin, mid_state, end_state))
+    ]
+    for store in stores:
+        store.start()
+    before0 = restricted(begin)
+    before1 = restricted(end_state)
     for j in range(GROUP - 1):
         arrive(f"side{j}")
     y = group[0]
@@ -798,15 +794,6 @@
     y = advance(y, MID - 2)[1:5] + group[3, 4:8]
     partial[...] = y
     start("part")
-    to_middle(7)
-    to_closing(8, None)
-    stores = [
-        pltpu.make_async_copy(field, fields_hbm.at[index], store_sem.at[3 + index])
-        for index, field in enumerate((begin, mid_state, end_state))
-    ]
-    for store in stores:
-        store.start()
-    before1 = restricted(end_state)
     arrive("flow2")
     arrive("flow3")
     lax.fori_loop(0, REACH - 1, coarse_coefficients, 0)
@@ -840,8 +827,6 @@
 
     for name in transfers:
         sent(name)
-    for piece in range(16):
-        pl.when(n < steps - 1)(lambda piece=piece: begin_copy(piece).wait_send())
     for k, d in enumerate((-1, 1)):
         for slot in range(4, 9):
             pl.when(has[d])(lambda k=k, d=d, slot=slot: fine_copy(k, d, slot).wait_send())
@@ -915,8 +900,8 @@
                 dma(2, 6),
                 pltpu.SemaphoreType.DMA,
                 pltpu.SemaphoreType.DMA,
-                dma(16),
-                dma(16),
+                pltpu.SemaphoreType.DMA,
+                pltpu.SemaphoreType.DMA,
                 dma(6),
                 dma(6),
                 dma(2, 2),

time: 65 us -> 69.1 us (1.063)
  the two profiles are of different devices: /device:TPU:104 before, /device:TPU:79 now
where the time goes in v8:
time: 69.1 us; the launch traced here: 68.9 us
  Pallas kernels  67 us (97%)
  other arithmetic  1.91 us (3%)
    pallas_call x1, Pallas kernels, body(): pl.pallas_call(functools.partial(kernel, steps, columns), out_shape=[jax....  67 us
    add x1, other arithmetic, body(): return (fields + lifted).reshape(1, 3, 64, ROWS, LANES)  1.91 us

profile of v8, /device:TPU:79, one launch (start us, length us, event | category | flops | bytes accessed | tf_op | source)
XLA Modules:
  0.0 68.9 jit_solution(15451719435380718936)
XLA Ops:
  0.0 67.0 %shard_map.37 = (f32[3,4,4,2,8,128]{5,4,3,2,1,0:T(8,128)}, f32[3,4,4,2,8,128]{5,4,3,2,1,0:T(8,128)}) custom-call(f32[3,4,4,2,8,128]{5,4,3,2,1,0:T(8,128)} %bitcast.4, f32[4,4,2,8,128]{4,3,2,1,0:T(8,128)} %bitcast.6, bf16[3,4,4,16,128]{4,3,2,1,0:T(8,128)(2,1)} %bitcast.5), custom_call_target="tpu_custom_call" | custom-call | tf_op jit(solution)/shard_map/pallas_call | solution.py:848
  67.0 1.9 %add.3 = f32[3,4,4,2,8,128]{5,4,3,2,1,0:T(8,128)} add(f32[3,4,4,2,8,128]{5,4,3,2,1,0:T(8,128)} %get-tuple-element.7, f32[3,4,4,2,8,128]{5,4,3,2,1,0:T(8,128)} %get-tuple-element.8) | non-fusion elementwise | flops 98304 | bytes 1179648 | tf_op jit(solution)/shard_map/add | solution.py:920

commit v9 on v8

--- a/solution.py
+++ b/solution.py
@@ -16,7 +16,7 @@
 DT = 0.5 * H
 LIFT = 6.0
 ROWS = 4
-REACH = 3
+REACH = 1
 SPAN = (2 * REACH + 1) * ROWS
 MID = REACH * ROWS
 FIELD = (4, 4, 2, 8, LANES)
@@ -100,8 +100,6 @@
     group,
     partial,
     near,
-    mid,
-    far,
     result,
     load_sem,
     store_sem,
@@ -256,21 +254,21 @@
         functools.partial(remote, leaving, passed, hop_send, hop_recv, (n + 1, s)),
         None,
     )
-    for index, d in enumerate((-3, -2, -1, 1, 2, 3)):
-        needed = None if abs(d) == 1 else g >= abs(d)
+    for index, d in enumerate((-1, 1)):
+        edge = pl.ds(0 if d < 0 else 1, ROWS - 1)
         add(
-            f"flow{abs(d)}",
-            both(needed, inside(d)),
-            both(needed, inside(-d)),
+            "flow",
+            has[d],
+            has[-d],
             functools.partial(
                 remote,
-                flows.at[REACH],
-                flows.at[REACH - d],
+                flows.at[REACH, edge],
+                flows.at[REACH - d, edge],
                 flow_send.at[index],
                 flow_recv.at[index],
                 (n, s + d),
             ),
-            (n, s - d),
+            None,
         )
     for shift in (1, 2, 3):
         add(
@@ -287,24 +285,21 @@
             ),
             (g * GROUP + (z + GROUP - shift) % GROUP, s),
         )
-    slot = 0
-    for distance, buffer in ((3, far), (2, mid), (1, near)):
-        for d in range(-distance, distance + 1):
-            add(
-                "part",
-                both(g + distance < groups, inside(d)),
-                both(g >= distance, inside(-d)),
-                functools.partial(
-                    remote,
-                    partial,
-                    buffer.at[pl.ds((distance - d) * ROWS, ROWS)],
-                    part_send.at[slot],
-                    part_recv.at[slot],
-                    (n + distance * GROUP, s + d),
-                ),
-                (n - distance * GROUP, s - d),
-            )
-            slot += 1
+    for d in (-1, 0, 1):
+        add(
+            "part",
+            both(g < groups - 1, inside(d)),
+            both(g > 0, inside(-d)),
+            functools.partial(
+                remote,
+                partial,
+                near.at[pl.ds((1 - d) * ROWS, ROWS)],
+                part_send.at[d + 1],
+                part_recv.at[d + 1],
+                (n + GROUP, s + d),
+            ),
+            (n - GROUP, s - d),
+        )
 
     def start(name):
         for sends, _, make, _ in transfers[name]:
@@ -335,8 +330,6 @@
     old1[...] = jnp.zeros(old1.shape, jnp.float32)
     group[...] = jnp.zeros(group.shape, jnp.float32)
     near[...] = jnp.zeros(near.shape, jnp.float32)
-    mid[...] = jnp.zeros(mid.shape, jnp.float32)
-    far[...] = jnp.zeros(far.shape, jnp.float32)
 
     barrier = pltpu.get_barrier_semaphore()
     expected = jnp.int32(0)
@@ -350,7 +343,7 @@
     for d in (-1, 1):
         greet(has[d], (n, s + d))
         expected = expected + has[d].astype(jnp.int32)
-    for name in ("begin_trace", "begin", "flow2", "flow3", "group", "part"):
+    for name in ("begin_trace", "begin", "group", "part"):
         for sends, receives, _, partner in transfers[name]:
             greet(receives, partner)
             expected = expected + (1 if sends is None else sends.astype(jnp.int32))
@@ -698,7 +691,7 @@
         duo_rates[x, 0] = duo_first[x]
         old0[x, 1 : ROWS + 1] = restricted(duo_begin.at[x])
     start("row0")
-    start("flow1")
+    start("flow")
     duo_middle(1)
     duo_closing(2)
 
@@ -756,7 +749,6 @@
     arrive("hop")
     group[z, pl.ds(ROWS, ROWS)] = offset + passed[...]
     start("group")
-    start("flow2")
 
     to_middle(7)
     for j in range(GROUP):
@@ -773,8 +765,7 @@
 
         if j < GROUP - 1:
             start(f"side{j}")
-    start("flow3")
-    arrive("flow1")
+    arrive("flow")
     coarse_coefficients(REACH - 1, 0)
     coarse_coefficients(REACH + 1, 0)
     to_closing(8, None)
@@ -788,30 +779,19 @@
     before1 = restricted(end_state)
     for j in range(GROUP - 1):
         arrive(f"side{j}")
-    y = group[0]
-    y = advance(y, MID - 4) + group[1, 1:11]
-    y = advance(y, MID - 3) + group[2, 2:10]
-    y = advance(y, MID - 2)[1:5] + group[3, 4:8]
+    arrive("part")
+    y = near[...]
+    line = [y[4:8]]
+    for j in range(GROUP):
+        y = advance(y, j) + group[j, j + 1 : 11 - j]
+        line.append(y[3 - j : 7 - j])
     partial[...] = y
     start("part")
-    arrive("flow2")
-    arrive("flow3")
-    lax.fori_loop(0, REACH - 1, coarse_coefficients, 0)
-    lax.fori_loop(REACH + 2, 2 * REACH + 1, coarse_coefficients, 0)
-    arrive("part")
-    y = far[...]
-    for step in range(4):
-        y = advance(y, step)
-    y = y + mid[...]
-    for step in range(4, 8):
-        y = advance(y, step)
-    y = y + near[...]
-    for j in range(3):
-        count = 12 - 2 * j
-        stepped = advance(y, MID - 4 + j) + group[j, j + 1 : 11 - j]
-        y = jnp.where(z > j, stepped, y[1 : count - 1])
-    finish = advance(y, MID - 1) + group[z, pl.ds(ROWS, ROWS)]
-    begin_rows = jnp.where(is_first, before0, y[1:5])
+    begin_rows, finish = line[0], line[1]
+    for j in range(1, GROUP):
+        begin_rows = jnp.where(z == j, line[j], begin_rows)
+        finish = jnp.where(z == j, line[j + 1], finish)
+    begin_rows = jnp.where(is_first, before0, begin_rows)
     delta0 = begin_rows - before0
     delta1 = finish - before1
 
@@ -889,8 +869,6 @@
                 vmem(GROUP, 3 * ROWS, 8, LANES),
                 vmem(ROWS, 8, LANES),
                 vmem(3 * ROWS, 8, LANES),
-                vmem(5 * ROWS, 8, LANES),
-                vmem(7 * ROWS, 8, LANES),
                 vmem(3, *FIELD),
                 dma(3),
                 dma(6),
@@ -902,16 +880,16 @@
                 pltpu.SemaphoreType.DMA,
                 pltpu.SemaphoreType.DMA,
                 pltpu.SemaphoreType.DMA,
-                dma(6),
-                dma(6),
+                dma(2),
+                dma(2),
                 dma(2, 2),
                 dma(2, 2),
                 dma(3),
                 dma(3),
                 dma(2, GROUP),
                 dma(2, GROUP),
-                dma(15),
-                dma(15),
+                dma(3),
+                dma(3),
             ],
             compiler_params=pltpu.CompilerParams(
                 collective_id=0, has_side_effects=True, vmem_limit_bytes=60 * 1024 * 1024

time: 69.1 us -> 74 us (1.071)
  the two profiles are of different devices: /device:TPU:79 before, /device:TPU:95 now
where the time goes in v9:
time: 74 us; the launch traced here: 73.8 us
  Pallas kernels  71.9 us (97%)
  other arithmetic  1.91 us (3%)
    pallas_call x1, Pallas kernels, body(): pl.pallas_call(functools.partial(kernel, steps, columns), out_shape=[jax....  71.9 us
    add x1, other arithmetic, body(): return (fields + lifted).reshape(1, 3, 64, ROWS, LANES)  1.91 us

profile of v9, /device:TPU:95, one launch (start us, length us, event | category | flops | bytes accessed | tf_op | source)
XLA Modules:
  0.0 73.8 jit_solution(12540788561418432540)
XLA Ops:
  0.0 71.9 %shard_map.37 = (f32[3,4,4,2,8,128]{5,4,3,2,1,0:T(8,128)}, f32[3,4,4,2,8,128]{5,4,3,2,1,0:T(8,128)}) custom-call(f32[3,4,4,2,8,128]{5,4,3,2,1,0:T(8,128)} %bitcast.4, f32[4,4,2,8,128]{4,3,2,1,0:T(8,128)} %bitcast.6, bf16[3,4,4,16,128]{4,3,2,1,0:T(8,128)(2,1)} %bitcast.5), custom_call_target="tpu_custom_call" | custom-call | tf_op jit(solution)/shard_map/pallas_call | solution.py:828
  71.9 1.9 %add.3 = f32[3,4,4,2,8,128]{5,4,3,2,1,0:T(8,128)} add(f32[3,4,4,2,8,128]{5,4,3,2,1,0:T(8,128)} %get-tuple-element.7, f32[3,4,4,2,8,128]{5,4,3,2,1,0:T(8,128)} %get-tuple-element.8) | non-fusion elementwise | flops 98304 | bytes 1179648 | tf_op jit(solution)/shard_map/add | solution.py:898

commit v10 on v7

--- a/solution.py
+++ b/solution.py
@@ -769,8 +769,6 @@
     to_closing(4, 5)
     rates[0] = first_rate[...]
     before0 = restricted(begin)
-
-    to_middle(5)
     for j in range(GROUP):
 
         @pl.when(z != j)
@@ -789,7 +787,7 @@
     arrive("flow1")
     coarse_coefficients(REACH - 1, 0)
     coarse_coefficients(REACH + 1, 0)
-    to_closing(6, 7)
+    to_middle(5)
     for j in range(GROUP - 1):
         arrive(f"side{j}")
     y = group[0]
@@ -798,6 +796,7 @@
     y = advance(y, MID - 2)[1:5] + group[3, 4:8]
     partial[...] = y
     start("part")
+    to_closing(6, 7)
     to_middle(7)
     to_closing(8, None)
     stores = [

time: 65 us -> 68.4 us (1.052)
  the two profiles are of different devices: /device:TPU:104 before, /device:TPU:39 now
where the time goes in v10:
time: 68.4 us; the launch traced here: 68.2 us
  Pallas kernels  66.3 us (97%)
  other arithmetic  1.91 us (3%)
    pallas_call x1, Pallas kernels, body(): pl.pallas_call(functools.partial(kernel, steps, columns), out_shape=[jax....  66.3 us
    add x1, other arithmetic, body(): return (fields + lifted).reshape(1, 3, 64, ROWS, LANES)  1.91 us

profile of v10, /device:TPU:39, one launch (start us, length us, event | category | flops | bytes accessed | tf_op | source)
XLA Modules:
  0.0 68.2 jit_solution(4047274628632009107)
XLA Ops:
  0.0 66.3 %shard_map.37 = (f32[3,4,4,2,8,128]{5,4,3,2,1,0:T(8,128)}, f32[3,4,4,2,8,128]{5,4,3,2,1,0:T(8,128)}) custom-call(f32[3,4,4,2,8,128]{5,4,3,2,1,0:T(8,128)} %bitcast.4, f32[4,4,2,8,128]{4,3,2,1,0:T(8,128)} %bitcast.6, bf16[3,4,4,16,128]{4,3,2,1,0:T(8,128)(2,1)} %bitcast.5), custom_call_target="tpu_custom_call" | custom-call | tf_op jit(solution)/shard_map/pallas_call | solution.py:862
  66.3 1.9 %add.3 = f32[3,4,4,2,8,128]{5,4,3,2,1,0:T(8,128)} add(f32[3,4,4,2,8,128]{5,4,3,2,1,0:T(8,128)} %get-tuple-element.7, f32[3,4,4,2,8,128]{5,4,3,2,1,0:T(8,128)} %get-tuple-element.8) | non-fusion elementwise | flops 98304 | bytes 1179648 | tf_op jit(solution)/shard_map/add | solution.py:934
